TPU v7x, 32 devices: a whole 2x2x4 slice. The times are simulated.
32 devices in a mesh: ctx: 4 (over x, core), tp: 4 (over z), dp: 2 (over y).
Axes of the slice: x: 2, y: 2, z: 4, core: 2. Of those that a mesh axis runs over, the one named last changes fastest.
Arguments:
- activations: bfloat16 [4096, 4096], P(('ctx', 'tp', 'dp')), may hold values from -6 to 6
- out_grad: bfloat16 [4096, 4096], P(('ctx', 'tp', 'dp')), may hold values from -6 to 6
- routes: int32 [4096, 8], P(('ctx', 'tp', 'dp')), may hold values from 0 to 31, all different within a row; in each aligned block of 128 rows (0 to 127, 128 to 255, ...) at most 48 rows name the same one
- gate_probs: bfloat16 [4096, 8], P(('ctx', 'tp', 'dp')), may hold values from 0.049804688 to 0.59765625
- saved_pre: bfloat16 [16, 2, 768, 1536], P(('ctx', 'tp'), 'dp'), may hold values from -6 to 6
- expert_weights: bfloat16 [16, 4096, 2304], P(('ctx', 'tp'), 'dp'), may hold values from -0.09375 to 0.09375
Outputs:
- input_grad: bfloat16 [4096, 4096], P(('ctx', 'tp', 'dp'))
- prob_grad: bfloat16 [4096, 8], P(('ctx', 'tp', 'dp'))
- weight_grad: bfloat16 [16, 4096, 2304], P(('ctx', 'tp'), 'dp')
Inputs may be any that keep to these rules, and one draw needn't show every extreme that they name: `routes`: each row names 8 different experts. Within the rows of one device (aligned blocks of 128 rows) no expert is named more than 48 times, a bound that some block reaches.
All inputs are finite; a program needn't handle non-finite values.
Results may differ from a plain program's by a relative error of at most 0.02.
Values may be sent and summed in bfloat16 or wider, within the bound.
A program may use at most 192 MiB of HBM per device.

v0:
```python
import jax
import jax.numpy as jnp
from jax import lax
from jax.sharding import PartitionSpec as P


def body(activations, out_grad, routes, gate_probs, saved_pre, expert_weights):
    tok_count = activations.shape[0]
    top_k = routes.shape[1]
    model_width = activations.shape[1]
    ctx_size = lax.axis_size("ctx")
    tp_size = lax.axis_size("tp")
    sources = ctx_size * tp_size
    slots_all = saved_pre.shape[2]
    capacity = slots_all // sources
    hidden = saved_pre.shape[3] // 2
    flat_routes = routes.reshape(-1)
    in_window = flat_routes < sources
    onehot = (flat_routes[:, None] == jnp.arange(sources, dtype=jnp.int32)[None, :]).astype(
        jnp.int32
    )
    position = jnp.sum(jnp.cumsum(onehot, axis=0) * onehot, axis=1) - 1
    slot_index = jnp.where(in_window, flat_routes * capacity + position, sources * capacity)
    route_count = tok_count * top_k
    route_of_slot = jnp.full((sources * capacity,), route_count, jnp.int32)
    route_of_slot = route_of_slot.at[slot_index].set(
        jnp.arange(route_count, dtype=jnp.int32), mode="drop"
    )
    filled = route_of_slot < route_count
    safe_route = jnp.minimum(route_of_slot, route_count - 1)
    token_of_slot = safe_route // top_k
    zero_value = jnp.zeros((), jnp.bfloat16)
    send_rows = jnp.where(filled[:, None], activations[token_of_slot], zero_value)
    send_grads = jnp.where(filled[:, None], out_grad[token_of_slot], zero_value)
    send_probs = jnp.where(filled, gate_probs.reshape(-1)[safe_route], zero_value)
    received = (
        lax.all_to_all(
            send_rows.reshape(sources, capacity, model_width),
            ("ctx", "tp"),
            split_axis=0,
            concat_axis=0,
            tiled=True,
        ),
        lax.all_to_all(
            send_grads.reshape(sources, capacity, model_width),
            ("ctx", "tp"),
            split_axis=0,
            concat_axis=0,
            tiled=True,
        ),
        lax.all_to_all(
            send_probs.reshape(sources, capacity),
            ("ctx", "tp"),
            split_axis=0,
            concat_axis=0,
            tiled=True,
        ),
    )
    recv_rows = received[0].reshape(slots_all, model_width)
    recv_grads = received[1].reshape(slots_all, model_width)
    prob_column = received[2].reshape(slots_all, 1).astype(jnp.float32)
    saved_rows = saved_pre[0, 0]
    pre_gate = saved_rows[:, :hidden].astype(jnp.float32)
    pre_up = saved_rows[:, hidden:].astype(jnp.float32)
    sigmoid_gate = jax.nn.sigmoid(pre_gate)
    activated = pre_gate * sigmoid_gate
    hidden_act = activated * pre_up
    weights = expert_weights[0]
    down_part = weights[:, 2 * hidden :]
    gate_up_part = weights[:, : 2 * hidden]
    down_grad = jnp.dot(
        recv_grads,
        lax.all_gather(down_part, "dp", axis=0, tiled=True),
        preferred_element_type=jnp.float32,
    )
    prob_slot = jnp.sum(hidden_act * down_grad, axis=1).astype(jnp.bfloat16)
    scaled_grad = prob_column * down_grad
    finish_gate_up_grad = jnp.concatenate(
        [
            scaled_grad * pre_up * sigmoid_gate * (1.0 + pre_gate * (1.0 - sigmoid_gate)),
            scaled_grad * activated,
        ],
        axis=1,
    ).astype(jnp.bfloat16)
    finish_scaled_hidden = (prob_column * hidden_act).astype(jnp.bfloat16)
    prob_slot, gate_up_grad, scaled_hidden = (prob_slot, finish_gate_up_grad, finish_scaled_hidden)
    row_grad = lax.dot_general(
        gate_up_grad,
        lax.all_gather(gate_up_part, "dp", axis=0, tiled=True),
        (((1,), (1,)), ((), ())),
        preferred_element_type=jnp.float32,
    ).astype(jnp.bfloat16)
    gate_up_term = lax.dot_general(
        recv_rows, gate_up_grad, (((0,), (0,)), ((), ())), preferred_element_type=jnp.float32
    )
    down_piece = lax.dot_general(
        recv_grads, scaled_hidden, (((0,), (0,)), ((), ())), preferred_element_type=jnp.float32
    )
    weight_grad = lax.psum_scatter(
        jnp.concatenate([gate_up_term, down_piece], axis=1).astype(jnp.bfloat16),
        "dp",
        scatter_dimension=0,
        tiled=True,
    )[None]
    returned = (
        lax.all_to_all(
            row_grad.reshape(sources, capacity, model_width),
            ("ctx", "tp"),
            split_axis=0,
            concat_axis=0,
            tiled=True,
        ),
        lax.all_to_all(
            prob_slot.reshape(sources, capacity),
            ("ctx", "tp"),
            split_axis=0,
            concat_axis=0,
            tiled=True,
        ),
    )
    back_rows = returned[0].reshape(sources * capacity, model_width)
    back_probs = returned[1].reshape(sources * capacity)
    safe_slot = jnp.minimum(slot_index, sources * capacity - 1)
    picked = jnp.where(in_window[:, None], back_rows[safe_slot], zero_value)
    input_grad = jnp.sum(picked.reshape(tok_count, top_k, model_width).astype(jnp.float32), axis=1)
    prob_grad = jnp.where(in_window, back_probs[safe_slot], zero_value).reshape(tok_count, top_k)
    return (input_grad.astype(jnp.bfloat16), prob_grad, weight_grad)


def solution(mesh):
    placed = (
        P(("ctx", "tp", "dp"), None),
        P(("ctx", "tp", "dp"), None),
        P(("ctx", "tp", "dp"), None),
        P(("ctx", "tp", "dp"), None),
        P(("ctx", "tp"), "dp", None, None),
        P(("ctx", "tp"), "dp", None),
    )
    return jax.shard_map(
        body,
        mesh=mesh,
        in_specs=placed,
        out_specs=(
            P(("ctx", "tp", "dp"), None),
            P(("ctx", "tp", "dp"), None),
            P(("ctx", "tp"), "dp", None),
        ),
        check_vma=False,
    )
```

profile of v0, /device:TPU:0, one launch (start us, length us, event | category | flops | bytes accessed | tf_op | source)
XLA Modules:
  0.0 603.1 jit_solution(2876701581721504563)
XLA Ops:
  7.2 0.8 broadcast_multiply_fusion
  8.0 0.8 copy.24
  8.7 0.1 eq.29
  8.8 0.1 eq.25
  9.0 0.8 copy.30
  9.8 0.1 reshape.169
  9.9 0.1 copy.25
  10.0 0.1 mul.63
  10.1 0.1 lt.57
  10.2 4.5 reduce-window.6
  14.7 0.1 slice.34
  14.8 0.1 copy.28
  15.0 0.1 broadcast_add_fusion
  15.2 4.3 scatter_custom_fusion
  19.6 5.0 gather_fusion
  24.6 0.7 all_to_all.25
  25.3 7.4 %all-to-all-start = ((bf16[16,1,48]{2,1,0:T(2,128)(2,1)}), bf16[16,1,48]{2,1,0:T(2,128)(2,1)S(1)}, u32[]{:S(2)}, u32[]{:S(2)}) async-start(bf16[16,1,48]{2,1,0:T(2,128)(2,1)} %all_to_all.25), calls=%async_computation | async-start | bytes 16384 | tf_op jit(solution)/shard_map/all_to_all | solution.py:51
  32.6 0.1 broadcast_in_dim.63
  32.7 5.7 gather_fusion.4
  38.4 5.7 gather_fusion.1
  44.1 10.3 %broadcast_select_fusion = (bf16[16,48,4096]{2,1,0:T(8,128)(2,1)}, bf16[16,48,4096]{2,1,0:T(8,128)(2,1)}) fusion(bf16[16,48,4096]{2,1,0:T(8,128)(2,1)} %bitcast.36, pred[16,48]{1,0:T(8,128)(4,1)S(1)} %broadcast_in_dim.63, bf16[16,48,4096]{2,1,0:T(8,128)(2,1)} %bitcast.37), kind=kLoop, calls=%fused_computation.12 | loop fusion | flops 6291456 | bytes 25166592 | tf_op jit(solution)/shard_map/jit(_where)/select_n | solution.py:33
  54.4 6.1 %all-to-all-start.1 = ((bf16[16,48,4096]{2,1,0:T(8,128)(2,1)}), bf16[16,48,4096]{2,1,0:T(8,128)(2,1)}, u32[]{:S(2)}, u32[]{:S(2)}) async-start(bf16[16,48,4096]{2,1,0:T(8,128)(2,1)} %get-tuple-element.22), calls=%async_computation.1 | async-start | bytes 12582912 | tf_op jit(solution)/shard_map/all_to_all | solution.py:44
  60.5 3.8 slice.36
  64.4 135.5 %all-to-all-done.1 = bf16[16,48,4096]{2,1,0:T(8,128)(2,1)} async-done(((bf16[16,48,4096]{2,1,0:T(8,128)(2,1)}), bf16[16,48,4096]{2,1,0:T(8,128)(2,1)}, u32[]{:S(2)}, u32[]{:S(2)}) %all-to-all-start.1) | async-done | bytes 6291488 | tf_op jit(solution)/shard_map/all_to_all | solution.py:44
  199.9 4.7 all-to-all-start.4
  204.6 5.9 slice.39
  210.5 0.2 reduce-scatter.2.cloned.1.call-start
  210.7 1.4 copy-done.3
  212.1 2.5 copy.32
  214.6 0.1 reshape.175
  214.7 10.4 %convolution_convert_fusion.1 = bf16[4096,768]{0,1:T(8,128)(2,1)} fusion(bf16[768,4096]{1,0:T(8,128)(2,1)} %bitcast.5, f32[768]{0:T(1024)S(1)} %reshape.175, bf16[768,1536]{0,1:T(8,128)(2,1)} %bitcast.42), kind=kOutput, calls=%fused_computation.10 | convolution fusion | flops 4840292352 | bytes 14945280 | tf_op jit(solution)/shard_map/dot_general | solution.py:96
  225.1 11.9 %fusion.3 = (bf16[768,768]{0,1:T(8,128)(2,1)}, bf16[768,768]{0,1:T(8,128)(2,1)}, bf16[768]{0:T(1024)(128)(2,1)S(1)}) fusion(f32[768]{0:T(1024)S(1)} %reshape.175, bf16[768,1536]{0,1:T(8,128)(2,1)S(1)} %bitcast.43, bf16[768,4096]{1,0:T(8,128)(2,1)} %bitcast.5, bf16[4096,768]{1,0:T(8,128)(2,1)} %all-gather.3.cloned.1.call-done), kind=kOutput, calls=%fused_computation.21 | convolution fusion | flops 4843043840 | bytes 17306112 | tf_op jit(solution)/shard_map/dot_general | solution.py:71
  237.1 106.8 %all-to-all-done.4 = bf16[16,48,4096]{2,1,0:T(8,128)(2,1)} async-done(((bf16[16,48,4096]{2,1,0:T(8,128)(2,1)}), bf16[16,48,4096]{2,1,0:T(8,128)(2,1)}, u32[]{:S(2)}, u32[]{:S(2)}) %all-to-all-start.4) | async-done | bytes 6291488 | tf_op jit(solution)/shard_map/all_to_all | solution.py:37
  343.8 12.8 %convolution_convert_fusion = bf16[4096,1536]{0,1:T(8,128)(2,1)S(1)} fusion(bf16[768,4096]{1,0:T(8,128)(2,1)} %bitcast.13, bf16[768,768]{0,1:T(8,128)(2,1)} %get-tuple-element.15, bf16[768,768]{0,1:T(8,128)(2,1)} %get-tuple-element.14), kind=kOutput, calls=%fused_computation.7 | convolution fusion | flops 9674686464 | bytes 21233664 | tf_op jit(solution)/shard_map/dot_general | solution.py:93
  356.6 16.8 %pad_maximum_fusion = bf16[4096,2304]{0,1:T(8,128)(2,1)} fusion(bf16[4096,768]{0,1:T(8,128)(2,1)} %convolution_convert_fusion.1, bf16[4096,1536]{0,1:T(8,128)(2,1)S(1)} %convolution_convert_fusion), kind=kLoop, calls=%fused_computation.6 | loop fusion | flops 37748736 | bytes 37748736 | tf_op jit(solution)/shard_map/concatenate | solution.py:100
  373.5 0.7 convert_element_type.56
  374.1 3.8 all-to-all-start.3
  378.0 15.0 %convolution_convert_fusion.2 = bf16[768,4096]{1,0:T(8,128)(2,1)} fusion(bf16[4096,1536]{1,0:T(8,128)(2,1)} %all-gather.5.cloned.1.call-done, bf16[768,768]{0,1:T(8,128)(2,1)S(1)} %copy-done.8, bf16[768,768]{0,1:T(8,128)(2,1)S(1)} %copy-done.7), kind=kOutput, calls=%fused_computation.11 | convolution fusion | flops 9671540736 | bytes 21233664 | tf_op jit(solution)/shard_map/dot_general | solution.py:87
  393.0 5.9 all-to-all-start.2
  399.0 0.1 reshape.173
  399.1 6.8 %gather_fusion.3 = bf16[1024]{0:T(1024)(128)(2,1)S(1)} fusion(bf16[768]{0:T(1024)(128)(2,1)S(1)} %reshape.173, s32[1024]{0:T(1024)S(1)} %broadcast_clamp_fusion), kind=kCustom, calls=%fused_computation.3 | custom fusion | bytes 8192 | tf_op jit(solution)/shard_map/gather | solution.py:126
  405.9 0.1 gather.29
  406.0 0.7 copy.34
  406.6 131.7 %all-to-all-done.2 = bf16[16,48,4096]{2,1,0:T(8,128)(2,1)} async-done(((bf16[16,48,4096]{2,1,0:T(8,128)(2,1)}), bf16[16,48,4096]{2,1,0:T(8,128)(2,1)}, u32[]{:S(2)}, u32[]{:S(2)}) %all-to-all-start.2) | async-done | bytes 6291488 | tf_op jit(solution)/shard_map/all_to_all | solution.py:106
  538.3 19.0 %gather_fusion.2 = bf16[1024,4096]{1,0:T(8,128)(2,1)} fusion(bf16[768,4096]{1,0:T(8,128)(2,1)} %bitcast.9, s32[1024]{0:T(1024)S(1)} %broadcast_clamp_fusion), kind=kCustom, calls=%fused_computation.2 | custom fusion | bytes 16781312 | tf_op jit(solution)/shard_map/gather | solution.py:124
  557.3 8.8 %fusion = bf16[128,4096]{1,0:T(8,128)(2,1)} fusion(bf16[1024,4096]{1,0:T(8,128)(2,1)} %gather_fusion.2, pred[128,8]{1,0:T(8,128)(4,1)S(1)} %copy-done.6), kind=kLoop, calls=%fused_computation.9 | loop fusion | flops 7864320 | bytes 9438208 | tf_op jit(solution)/shard_map/reduce_sum | solution.py:125
  566.1 17.8 %reduce-scatter.2.cloned.1.call-done = bf16[2048,2304]{0,1:T(8,128)(2,1)} async-done(((bf16[4096,2304]{0,1:T(8,128)(2,1)}), bf16[2048,2304]{0,1:T(8,128)(2,1)}) %reduce-scatter.2.cloned.1.call-update) | async-done | bytes 9437200 | tf_op jit(solution)/shard_map/reduce_scatter | solution.py:99
  583.9 12.7 %copy.35 = bf16[1,2048,2304]{2,1,0:T(8,128)(2,1)} copy(bf16[1,2048,2304]{1,2,0:T(8,128)(2,1)} %bitcast.40) | data formatting | bytes 18874368
  (42 shorter events, 0.5 us)
Async XLA Ops:
  7.2 25.6 %copy-start = (bf16[128,4096]{1,0:T(8,128)(2,1)S(1)}, bf16[128,4096]{1,0:T(8,128)(2,1)}, u32[]{:S(2)}) copy-start(bf16[128,4096]{1,0:T(8,128)(2,1)} %param.6) | copy-start | bytes 3145732
  9.0 1.1 copy-start.5
  25.3 29.1 %all-to-all-start = ((bf16[16,1,48]{2,1,0:T(2,128)(2,1)}), bf16[16,1,48]{2,1,0:T(2,128)(2,1)S(1)}, u32[]{:S(2)}, u32[]{:S(2)}) async-start(bf16[16,1,48]{2,1,0:T(2,128)(2,1)} %all_to_all.25), calls=%async_computation | async-start | bytes 16384 | tf_op jit(solution)/shard_map/all_to_all | solution.py:51
  32.7 5.7 copy-start.2
  54.4 145.4 %all-to-all-start.1 = ((bf16[16,48,4096]{2,1,0:T(8,128)(2,1)}), bf16[16,48,4096]{2,1,0:T(8,128)(2,1)}, u32[]{:S(2)}, u32[]{:S(2)}) async-start(bf16[16,48,4096]{2,1,0:T(8,128)(2,1)} %get-tuple-element.22), calls=%async_computation.1 | async-start | bytes 12582912 | tf_op jit(solution)/shard_map/all_to_all | solution.py:44
  60.5 164.7 %all-gather.3.cloned.1.call-start = ((), (), s32[]{:S(2)}) async-start(), calls=%async_computation.6 | async-start | bytes 9437184 | tf_op jit(solution)/shard_map/all_gather | solution.py:73
  199.9 144.0 %all-to-all-start.4 = ((bf16[16,48,4096]{2,1,0:T(8,128)(2,1)}), bf16[16,48,4096]{2,1,0:T(8,128)(2,1)}, u32[]{:S(2)}, u32[]{:S(2)}) async-start(bf16[16,48,4096]{2,1,0:T(8,128)(2,1)} %get-tuple-element.21), calls=%async_computation.4 | async-start | bytes 12582912 | tf_op jit(solution)/shard_map/all_to_all | solution.py:37
  204.5 173.4 %all-gather.5.cloned.1.call-start = ((), (), s32[]{:S(2)}) async-start(), calls=%async_computation.7 | async-start | bytes 18874368 | tf_op jit(solution)/shard_map/all_gather | solution.py:89
  210.5 1.7 copy-start.3
  210.5 373.4 %reduce-scatter.2.cloned.1.call-start = ((), (), s32[]{:S(2)}) async-start(), calls=%async_computation.8 | async-start | bytes 28311552 | tf_op jit(solution)/shard_map/reduce_scatter | solution.py:99
  214.7 10.4 %copy-start.4 = (bf16[1,1,768,1536]{2,3,1,0:T(8,128)(2,1)S(1)}, bf16[1,1,768,1536]{2,3,1,0:T(8,128)(2,1)}, u32[]{:S(2)}) copy-start(bf16[1,1,768,1536]{2,3,1,0:T(8,128)(2,1)} %copy.32) | copy-start | bytes 7077892
  373.4 4.5 copy-start.7
  373.4 4.5 copy-start.8
  374.1 18.9 %all-to-all-start.3 = ((bf16[16,1,48]{2,1,0:T(2,128)(2,1)}), bf16[16,1,48]{2,1,0:T(2,128)(2,1)S(1)}, u32[]{:S(2)}, u32[]{:S(2)}) async-start(bf16[16,1,48]{2,1,0:T(2,128)(2,1)} %convert_element_type.56), calls=%async_computation.3 | async-start | bytes 16384 | tf_op jit(solution)/shard_map/all_to_all | solution.py:113
  393.0 145.3 %all-to-all-start.2 = ((bf16[16,48,4096]{2,1,0:T(8,128)(2,1)}), bf16[16,48,4096]{2,1,0:T(8,128)(2,1)}, u32[]{:S(2)}, u32[]{:S(2)}) async-start(bf16[16,48,4096]{2,1,0:T(8,128)(2,1)} %bitcast.41), calls=%async_computation.2 | async-start | bytes 12582912 | tf_op jit(solution)/shard_map/all_to_all | solution.py:106
  538.3 19.0 %copy-start.6 = (pred[128,8]{1,0:T(8,128)(4,1)S(1)}, pred[128,8]{1,0:T(8,128)(4,1)}, u32[]{:S(2)}) copy-start(pred[128,8]{1,0:T(8,128)(4,1)} %copy-done.5) | copy-start | bytes 3076
  583.9 12.7 %copy-start.1 = (bf16[128,4096]{1,0:T(8,128)(2,1)S(1)}, bf16[128,4096]{1,0:T(8,128)(2,1)}, u32[]{:S(2)}) copy-start(bf16[128,4096]{1,0:T(8,128)(2,1)} %param.6) | copy-start | bytes 3145732
Sparse Core Ops, SparseCore 0:
  64.5 81.6 all-gather.2
  210.6 153.7 all-gather.4
  373.6 210.2 reduce-scatter.1
where the time goes:
time: 604 us; the launch traced here: 603 us
  waiting for transfers between devices  392 us (65%)
  local copies, waits for them, and re-layouts  77.6 us (13%)
  matrix products  50.1 us (8%)
  other arithmetic  41.5 us (7%)
  starting transfers between devices  28.1 us (5%)
  between operations  14 us (2%)
    all_to_all x1, waiting for transfers between devices, body(): lax.all_to_all(send_grads.reshape(sources, capacity, model_width), ('ctx'...  135 us
    all_to_all x1, waiting for transfers between devices, body(): lax.all_to_all(row_grad.reshape(sources, capacity, model_width), ('ctx',...  132 us
    all_to_all x1, waiting for transfers between devices, body(): lax.all_to_all(send_rows.reshape(sources, capacity, model_width), ('ctx',...  107 us
    gather x1, local copies, waits for them, and re-layouts, body(): picked = jnp.where(in_window[:, None], back_rows[safe_slot], zero_value)  19 us
    unnamed x23, local copies, waits for them, and re-layouts  18.9 us
    reduce_scatter x1, waiting for transfers between devices, body(): lax.psum_scatter(jnp.concatenate([gate_up_term, down_piece], axis=1).asty...  17.8 us
    concatenate x1, other arithmetic, body(): jnp.concatenate([gate_up_term, down_piece], axis=1).astype(jnp.bfloat16)  16.8 us
    dot_general x1, matrix products, body(): lax.dot_general(gate_up_grad, lax.all_gather(gate_up_part, 'dp', axis=0,...  15 us
  transfers between devices with their start and end apart: 8, of which 4 were waited for; matrix products, arithmetic and copies ran while one was open for 23% of the time, Pallas kernels for 0%

commit v1 on v0

v1 whole, which is shorter than its diff:
```python
import jax
import jax.numpy as jnp
from jax import lax
from jax.sharding import PartitionSpec as P

PLANE = ("ctx", "tp")
F32 = jnp.float32
BF16 = jnp.bfloat16


def gather_plane(x):
    return lax.all_gather(x, PLANE, axis=0, tiled=False)


def scatter_plane(x):
    return lax.psum_scatter(x, PLANE, scatter_dimension=0, tiled=False)


def body(activations, out_grad, routes, gate_probs, saved_pre, expert_weights):
    tokens, width = activations.shape
    top_k = routes.shape[1]
    sources = lax.axis_size("ctx") * lax.axis_size("tp")
    expert = lax.axis_index(PLANE)
    replica = lax.axis_index("dp")
    slots = saved_pre.shape[2]
    cap = slots // sources
    hidden = saved_pre.shape[3] // 2
    half = width // 2
    swap = [(0, 1), (1, 0)]

    def halves(x):
        low, high = x[:, :half], x[:, half:]
        keep = jnp.where(replica == 0, low, high)
        give = jnp.where(replica == 0, high, low)
        return keep, give

    grad_keep, grad_give = halves(out_grad)
    act_keep, act_give = halves(activations)
    grad_other = lax.ppermute(grad_give, "dp", swap)
    act_other = lax.ppermute(act_give, "dp", swap)
    own_pre = saved_pre[0, 0]
    other_pre = lax.ppermute(own_pre, "dp", swap)

    routes_own = lax.all_gather(routes, PLANE, axis=0, tiled=False)
    probs_own = lax.all_gather(gate_probs, PLANE, axis=0, tiled=False)
    routes_other = lax.ppermute(routes_own, "dp", swap)
    probs_other = lax.ppermute(probs_own, "dp", swap)

    earlier = (
        lax.broadcasted_iota(jnp.int32, (tokens, tokens), 0)
        < lax.broadcasted_iota(jnp.int32, (tokens, tokens), 1)
    ).astype(BF16)

    def select(routes_in, probs_in):
        hit = routes_in == expert
        named = jnp.any(hit, axis=2)
        prob = jnp.sum(jnp.where(hit, probs_in.astype(F32), 0.0), axis=2)
        rank = jnp.dot(named.astype(BF16), earlier, preferred_element_type=F32)
        place = lax.broadcasted_iota(jnp.int32, (sources, cap, tokens), 1)
        chosen = named[:, None, :] & (rank.astype(jnp.int32)[:, None, :] == place)
        prob_column = jnp.sum(jnp.where(chosen, prob[:, None, :], 0.0), axis=2)
        return chosen.astype(BF16), prob_column.reshape(slots, 1)

    chosen = []
    columns = []
    for pair in ((routes_own, probs_own), (routes_other, probs_other)):
        c, p = select(*pair)
        chosen.append(c)
        columns.append(p)

    def pack(which, gathered):
        return jnp.einsum(
            "spt,std->spd", chosen[which], gathered, preferred_element_type=F32
        ).astype(BF16).reshape(slots, half)

    weights = expert_weights[0]
    down_part = weights[:, 2 * hidden :]
    gate_up_part = weights[:, : 2 * hidden]

    grad_rows = [pack(0, gather_plane(grad_keep)), pack(1, gather_plane(grad_other))]
    act_rows = [pack(0, gather_plane(act_keep)), pack(1, gather_plane(act_other))]
    part = [jnp.dot(g, down_part, preferred_element_type=F32) for g in grad_rows]
    arrived = [
        lax.ppermute(part[1].astype(BF16), "dp", swap),
        lax.ppermute(part[0].astype(BF16), "dp", swap),
    ]
    gate_up = []
    scaled = []
    token_probs = None
    for i, pre in enumerate((own_pre, other_pre)):
        down_grad = part[i] + arrived[i].astype(F32)
        gate = pre[:, :hidden].astype(F32)
        up = pre[:, hidden:].astype(F32)
        sig = jax.nn.sigmoid(gate)
        act = gate * sig
        hidden_act = act * up
        if i == 0:
            slot_prob = jnp.sum(hidden_act * down_grad, axis=1).astype(BF16)
            token_probs = jnp.sum(
                jnp.where(chosen[0] > 0, slot_prob.reshape(sources, cap, 1).astype(F32), 0.0),
                axis=1,
            ).astype(BF16)
        dh = columns[i] * down_grad
        gate_up.append(
            jnp.concatenate([dh * up * sig * (1.0 + gate * (1.0 - sig)), dh * act], axis=1).astype(
                BF16
            )
        )
        scaled.append((columns[i] * hidden_act).astype(BF16))

    summed = [None, None]
    for i in (1, 0):
        row_grad = lax.dot_general(
            gate_up[i], gate_up_part, (((1,), (1,)), ((), ())), preferred_element_type=F32
        ).astype(BF16)
        spread = jnp.einsum(
            "spt,spd->std",
            chosen[i],
            row_grad.reshape(sources, cap, half),
            preferred_element_type=F32,
        ).astype(BF16)
        summed[i] = scatter_plane(spread)

    def outer(rows, cols):
        return lax.dot_general(rows, cols, (((0,), (0,)), ((), ())), preferred_element_type=F32)

    gate_up_term = outer(act_rows[0], gate_up[0]) + outer(act_rows[1], gate_up[1])
    down_term = outer(grad_rows[0], scaled[0]) + outer(grad_rows[1], scaled[1])
    weight_grad = jnp.concatenate([gate_up_term.astype(BF16), down_term.astype(BF16)], axis=1)[None]

    far = lax.ppermute(summed[1], "dp", swap)
    near = summed[0]
    input_grad = jnp.concatenate(
        [jnp.where(replica == 0, near, far), jnp.where(replica == 0, far, near)], axis=1
    )
    back = lax.all_to_all(token_probs, PLANE, split_axis=0, concat_axis=0, tiled=True)
    experts = lax.broadcasted_iota(jnp.int32, (sources, tokens, top_k), 0)
    prob_grad = jnp.sum(
        jnp.where(routes[None] == experts, back[:, :, None].astype(F32), 0.0), axis=0
    ).astype(BF16)
    return (input_grad, prob_grad, weight_grad)


def solution(mesh):
    placed = (
        P(("ctx", "tp", "dp"), None),
        P(("ctx", "tp", "dp"), None),
        P(("ctx", "tp", "dp"), None),
        P(("ctx", "tp", "dp"), None),
        P(("ctx", "tp"), "dp", None, None),
        P(("ctx", "tp"), "dp", None),
    )
    return jax.shard_map(
        body,
        mesh=mesh,
        in_specs=placed,
        out_specs=(
            P(("ctx", "tp", "dp"), None),
            P(("ctx", "tp", "dp"), None),
            P(("ctx", "tp"), "dp", None),
        ),
        check_vma=False,
    )
```

time: 604 us -> 555 us (0.919)
  waiting for transfers between devices: 392 us -> 318 us
  blocking collectives: 0 us -> 61.4 us
  local copies, waits for them, and re-layouts: 77.6 us -> 19.8 us
  matrix products: 50.1 us -> 99.5 us
  other arithmetic: 41.5 us -> 24.8 us
  starting transfers between devices: 28.1 us -> 15.9 us
    all_to_all x5 -> x1, waiting for transfers between devices: 374 us -> 0.01 us  [body(): lax.all_to_all(token_probs, PLANE, split_axis=0, concat_axis=0, tiled=True)]
    reduce_scatter x1 -> x2, waiting for transfers between devices: 17.8 us -> 149 us  [scatter_plane(): return lax.psum_scatter(x, PLANE, scatter_dimension=0, tiled=False)]
    all_gather x2 -> x4, waiting for transfers between devices: 0.02 us -> 115 us  [gather_plane(): return lax.all_gather(x, PLANE, axis=0, tiled=False)]
    all_gather x0 -> x2, blocking collectives: none -> 61.4 us  [the longest x1 32.1 us: body(): routes_own = lax.all_gather(routes, PLANE, axis=0, tiled=False)]
    ppermute x0 -> x8, waiting for transfers between devices: none -> 53.2 us  [the longest x1 26.8 us: body(): lax.ppermute(part[0].astype(BF16), 'dp', swap)]
    dot_general x4 -> x16, matrix products: 50.1 us -> 99.5 us  [the longest x4 32.9 us: outer(): lax.dot_general(rows, cols, (((0,), (0,)), ((), ())), preferred_element_t...]
    gather x6 -> x0, local copies, waits for them, and re-layouts: 42.2 us -> none  [the longest x1 19 us: body(): picked = jnp.where(in_window[:, None], back_rows[safe_slot], zero_value)]
    all_to_all x5 -> x1, starting transfers between devices: 27.8 us -> 3.73 us  [body(): lax.all_to_all(token_probs, PLANE, split_axis=0, concat_axis=0, tiled=True)]
  transfers between devices with their start and end apart: 8 -> 15, of which waited for: 4 -> 8; matrix products, arithmetic and copies ran while one was open for 23% -> 25% of each run, Pallas kernels for 0% -> 0%
where the time goes in v1:
time: 555 us; the launch traced here: 554 us
  waiting for transfers between devices  318 us (57%)
  matrix products  99.5 us (18%)
  blocking collectives  61.4 us (11%)
  other arithmetic  24.8 us (4%)
  local copies, waits for them, and re-layouts  19.8 us (4%)
  starting transfers between devices  15.9 us (3%)
  between operations  14.3 us (3%)
    reduce_scatter x2, waiting for transfers between devices, scatter_plane(): return lax.psum_scatter(x, PLANE, scatter_dimension=0, tiled=False)  149 us
    all_gather x4, waiting for transfers between devices, gather_plane(): return lax.all_gather(x, PLANE, axis=0, tiled=False)  115 us
    dot_general x4, matrix products, outer(): lax.dot_general(rows, cols, (((0,), (0,)), ((), ())), preferred_element_t...  32.9 us
    all_gather x1, blocking collectives, body(): routes_own = lax.all_gather(routes, PLANE, axis=0, tiled=False)  32.1 us
    all_gather x1, blocking collectives, body(): probs_own = lax.all_gather(gate_probs, PLANE, axis=0, tiled=False)  29.3 us
    ppermute x1, waiting for transfers between devices, body(): lax.ppermute(part[0].astype(BF16), 'dp', swap)  26.8 us
    dot_general x4, matrix products, pack(): jnp.einsum('spt,std->spd', chosen[which], gathered, preferred_element_typ...  22.6 us
    unnamed x28, local copies, waits for them, and re-layouts  18.9 us
  transfers between devices with their start and end apart: 15, of which 8 were waited for; matrix products, arithmetic and copies ran while one was open for 25% of the time, Pallas kernels for 0%

profile of v1, /device:TPU:0, one launch (start us, length us, event | category | flops | bytes accessed | tf_op | source)
XLA Modules:
  0.0 554.1 jit_solution(2479780255174016591)
XLA Ops:
  7.2 2.1 broadcast_select_fusion.3
  9.4 3.0 collective-permute-start.1
  12.3 11.9 %collective-permute-done.1 = bf16[128,2048]{1,0:T(8,128)(2,1)S(1)} collective-permute-done((bf16[128,2048]{1,0:T(8,128)(2,1)S(1)}, bf16[128,2048]{1,0:T(8,128)(2,1)S(1)}, u32[]{:S(2)}, u32[]{:S(2)}) %collective-permute-start.1) | collective-permute-done | bytes 524320 | tf_op jit(solution)/shard_map/ppermute | solution.py:39
  24.3 0.8 copy-done.10
  25.1 0.7 all-gather.11.cloned.1.call-update
  25.9 0.9 broadcast_select_fusion
  26.8 1.8 collective-permute-start.7
  28.6 11.4 %collective-permute-done.7 = bf16[128,2048]{1,0:T(8,128)(2,1)S(1)} collective-permute-done((bf16[128,2048]{1,0:T(8,128)(2,1)S(1)}, bf16[128,2048]{1,0:T(8,128)(2,1)S(1)}, u32[]{:S(2)}, u32[]{:S(2)}) %collective-permute-start.7) | collective-permute-done | bytes 524320 | tf_op jit(solution)/shard_map/ppermute | solution.py:40
  40.0 0.8 copy-done.9
  40.9 32.1 %all-gather = s32[2048,8]{0,1:T(8,128)S(1)} all-gather(s32[128,8]{0,1:T(8,128)S(1)} %copy-done.11), channel_id=2, replica_groups=mesh['ctx'=4,'tp'=4,'dp'=2] {'ctx','tp'}, dimensions={0}, use_global_device_ids=true | all-gather | bytes 69632 | tf_op jit(solution)/shard_map/all_gather | solution.py:44
  73.0 1.4 collective-permute-start
  74.5 29.3 %all-gather.1 = bf16[2048,8]{0,1:T(8,128)(2,1)S(1)} all-gather(bf16[128,8]{0,1:T(8,128)(2,1)S(1)} %copy-done.12), channel_id=3, replica_groups=mesh['ctx'=4,'tp'=4,'dp'=2] {'ctx','tp'}, dimensions={0}, use_global_device_ids=true | all-gather | bytes 34816 | tf_op jit(solution)/shard_map/all_gather | solution.py:45
  103.7 0.8 collective-permute-start.3
  104.5 3.1 collective-permute-done.3
  107.8 4.7 convolution_convert_fusion.4
  112.6 6.4 %fusion.63 = (bf16[768,768]{0,1:T(8,128)(2,1)}, f32[768,768]{0,1:T(8,128)}) fusion(bf16[768,2048]{1,0:T(8,128)(2,1)S(1)} %bitcast.45, bf16[2048,2304]{1,0:T(8,128)(2,1)} %bitcast.61), kind=kOutput, calls=%fused_computation.102 | convolution fusion | flops 2416508928 | bytes 9830400 | tf_op jit(solution)/shard_map/dot_general | solution.py:82
  119.0 0.9 collective-permute-start.2
  119.8 4.3 copy.13
  124.1 1.2 collective-permute-start.5
  125.5 53.1 %all-gather.11.cloned.1.call-done = bf16[2048,2048]{1,0:T(8,128)(2,1)} async-done(((bf16[128,2048]{1,0:T(8,128)(2,1)}), bf16[2048,2048]{1,0:T(8,128)(2,1)}) %all-gather.11.cloned.1.call-update) | async-done | bytes 8388624 | tf_op jit(solution)/shard_map/all_gather | solution.py:12
  178.6 4.8 convolution_convert_fusion.5
  183.4 8.5 %multiply_reduce_fusion = (bf16[768]{0:T(1024)(128)(2,1)S(1)}, f32[768,768]{0,1:T(8,128)}) fusion(bf16[768,768]{0,1:T(8,128)(2,1)} %collective-permute-done.2, bf16[768,1536]{0,1:T(8,128)(2,1)S(1)} %bitcast.54, bf16[768,2048]{1,0:T(8,128)(2,1)S(1)} %bitcast.47, bf16[2048,2304]{1,0:T(8,128)(2,1)} %bitcast.62), kind=kOutput, calls=%fused_computation.48 | convolution fusion | flops 2422406400 | bytes 12191232 | tf_op jit(solution)/shard_map/dot_general | solution.py:82
  192.0 0.3 select_reduce_fusion
  192.4 6.5 %fusion.16 = (bf16[768,768]{0,1:T(8,128)(2,1)}, bf16[768,768]{0,1:T(8,128)(2,1)}, bf16[768,768]{0,1:T(8,128)(2,1)}) fusion(f32[768]{0:T(1024)S(1)} %mul.81, bf16[768,1536]{0,1:T(8,128)(2,1)} %bitcast.52, f32[768,768]{0,1:T(8,128)} %get-tuple-element.32, bf16[768,768]{0,1:T(8,128)(2,1)} %collective-permute-done.2), kind=kLoop, calls=%fused_computation.31 | loop fusion | flops 11206656 | bytes 9440256 | tf_op jit(solution)/shard_map/convert.4
  198.9 1.4 collective-permute-start.4
  200.6 26.8 %collective-permute-done.4 = bf16[768,768]{0,1:T(8,128)(2,1)} collective-permute-done((bf16[768,768]{0,1:T(8,128)(2,1)}, bf16[768,768]{0,1:T(8,128)(2,1)}, u32[]{:S(2)}, u32[]{:S(2)}) %collective-permute-start.4) | collective-permute-done | bytes 1179680 | tf_op jit(solution)/shard_map/ppermute | solution.py:85
  227.3 4.1 fusion.19
  231.4 9.4 %fusion.7 = bf16[768,2048]{1,0:T(8,128)(2,1)S(1)} fusion(bf16[2048,2304]{1,0:T(8,128)(2,1)} %bitcast.63, bf16[768,768]{0,1:T(8,128)(2,1)S(1)} %get-tuple-element.21, bf16[768,768]{0,1:T(8,128)(2,1)S(1)} %get-tuple-element.20), kind=kOutput, calls=%fused_computation.20 | convolution fusion | flops 4838129664 | bytes 11796480 | tf_op jit(solution)/shard_map/dot_general | solution.py:113
  240.8 5.8 %convolution_convert_fusion = bf16[16,128,2048]{2,1,0:T(8,128)(2,1)} fusion(bf16[16,48,2048]{2,1,0:T(8,128)(2,1)S(1)} %bitcast.55, s32[16,128]{1,0:T(8,128)S(1)} %convolution_convert_fusion.6, pred[16,128]{1,0:T(8,128)(4,1)S(1)} %reduce_or.19), kind=kOutput, calls=%fused_computation.7 | convolution fusion | flops 407044096 | bytes 11544576 | tf_op jit(solution)/shard_map/spt,spd->std/dot_general | solution.py:116
  246.7 8.0 %fusion.4 = bf16[768,2048]{1,0:T(8,128)(2,1)S(1)} fusion(bf16[2048,2304]{1,0:T(8,128)(2,1)} %bitcast.64, bf16[768,768]{0,1:T(8,128)(2,1)} %get-tuple-element.19, bf16[768,768]{0,1:T(8,128)(2,1)} %get-tuple-element.18), kind=kOutput, calls=%fused_computation.19 | convolution fusion | flops 4838129664 | bytes 11796480 | tf_op jit(solution)/shard_map/dot_general | solution.py:113
  254.7 5.6 %convolution_convert_fusion.1 = bf16[16,128,2048]{2,1,0:T(8,128)(2,1)} fusion(bf16[16,48,2048]{2,1,0:T(8,128)(2,1)S(1)} %bitcast.56, s32[16,128]{1,0:T(8,128)S(1)} %convolution_convert_fusion.7, pred[16,128]{1,0:T(8,128)(4,1)S(1)} %reduce_or.18), kind=kOutput, calls=%fused_computation.8 | convolution fusion | flops 407044096 | bytes 11544576 | tf_op jit(solution)/shard_map/spt,spd->std/dot_general | solution.py:116
  260.4 6.8 %convolution_convert_fusion.3 = bf16[16,48,2048]{2,1,0:T(8,128)(2,1)} fusion(bf16[16,128,2048]{2,1,0:T(8,128)(2,1)} %bitcast.41, s32[16,128]{1,0:T(8,128)S(1)} %convolution_convert_fusion.7, pred[16,128]{1,0:T(8,128)(4,1)S(1)} %reduce_or.18), kind=kOutput, calls=%fused_computation.16 | convolution fusion | flops 404422656 | bytes 11544576 | tf_op jit(solution)/shard_map/spt,std->spd/dot_general | solution.py:72
  267.1 62.1 %all-gather.17.cloned.1.call-done = bf16[2048,2048]{1,0:T(8,128)(2,1)} async-done(((bf16[128,2048]{1,0:T(8,128)(2,1)}), bf16[2048,2048]{1,0:T(8,128)(2,1)}) %all-gather.17.cloned.1.call-update) | async-done | bytes 8388624 | tf_op jit(solution)/shard_map/all_gather | solution.py:12
  329.2 6.4 %convolution_convert_fusion.2 = bf16[16,48,2048]{2,1,0:T(8,128)(2,1)} fusion(bf16[16,128,2048]{2,1,0:T(8,128)(2,1)} %bitcast.42, s32[16,128]{1,0:T(8,128)S(1)} %convolution_convert_fusion.6, pred[16,128]{1,0:T(8,128)(4,1)S(1)} %reduce_or.19), kind=kOutput, calls=%fused_computation.15 | convolution fusion | flops 404422656 | bytes 11544576 | tf_op jit(solution)/shard_map/spt,std->spd/dot_general | solution.py:72
  335.6 0.6 copy.14
  336.2 3.7 all-to-all-start
  339.9 6.0 %fusion.31 = f32[2048,768]{0,1:T(8,128)S(1)} fusion(bf16[768,2048]{1,0:T(8,128)(2,1)} %bitcast.48, f32[768]{0:T(1024)S(1)} %mul.81, bf16[768,1536]{0,1:T(8,128)(2,1)} %bitcast.53), kind=kOutput, calls=%fused_computation.54 | convolution fusion | flops 2421227520 | bytes 11799552 | tf_op jit(solution)/shard_map/dot_general | solution.py:125
  346.0 6.7 %add_convert_fusion.1 = bf16[2048,768]{0,1:T(8,128)(2,1)} fusion(f32[2048,768]{0,1:T(8,128)S(1)} %fusion.31, bf16[768,2048]{1,0:T(8,128)(2,1)S(1)} %bitcast.46, f32[768]{0:T(1024)S(1)} %mul.90, bf16[768,1536]{0,1:T(8,128)(2,1)} %collective-permute-done.5), kind=kOutput, calls=%fused_computation.2 | convolution fusion | flops 2424373248 | bytes 14945280 | tf_op jit(solution)/shard_map/dot_general | solution.py:125
  352.7 9.0 %fusion.30 = f32[2048,1536]{0,1:T(8,128)} fusion(bf16[768,2048]{1,0:T(8,128)(2,1)S(1)} %bitcast.50, bf16[768,768]{0,1:T(8,128)(2,1)S(1)} %copy-done.7, bf16[768,768]{0,1:T(8,128)(2,1)S(1)} %copy-done.6), kind=kOutput, calls=%fused_computation.53 | convolution fusion | flops 4836556800 | bytes 18087936 | tf_op jit(solution)/shard_map/dot_general | solution.py:125
  361.7 0.6 select_reduce_fusion.3
  362.3 11.2 %add_convert_fusion = bf16[2048,1536]{0,1:T(8,128)(2,1)} fusion(f32[2048,1536]{0,1:T(8,128)} %fusion.30, bf16[768,2048]{1,0:T(8,128)(2,1)S(1)} %bitcast.49, bf16[768,768]{0,1:T(8,128)(2,1)} %copy-done.5, bf16[768,768]{0,1:T(8,128)(2,1)} %copy-done.4), kind=kOutput, calls=%fused_computation | convolution fusion | flops 4842848256 | bytes 24379392 | tf_op jit(solution)/shard_map/dot_general | solution.py:125
  373.5 63.2 %reduce-scatter.5.cloned.1.call-done = bf16[1,128,2048]{2,1,0:T(8,128)(2,1)} async-done(((bf16[16,128,2048]{2,1,0:T(8,128)(2,1)}), bf16[1,128,2048]{2,1,0:T(8,128)(2,1)}) %reduce-scatter.5.cloned.1.call-update) | async-done | bytes 524304 | tf_op jit(solution)/shard_map/reduce_scatter | solution.py:16
  436.7 1.5 collective-permute-start.6
  438.2 7.8 %maximum_bitcast_fusion = bf16[1,2048,2304]{1,2,0:T(8,128)(2,1)} fusion(bf16[2048,768]{0,1:T(8,128)(2,1)} %add_convert_fusion.1, bf16[2048,1536]{0,1:T(8,128)(2,1)} %add_convert_fusion), kind=kLoop, calls=%fused_computation.1 | loop fusion | flops 18874368 | bytes 18874368 | tf_op jit(solution)/shard_map/broadcast_in_dim | solution.py:129
  445.9 13.0 %copy.15 = bf16[1,2048,2304]{2,1,0:T(8,128)(2,1)} copy(bf16[1,2048,2304]{1,2,0:T(8,128)(2,1)} %maximum_bitcast_fusion) | data formatting | bytes 18874368
  459.0 86.1 %reduce-scatter.3.cloned.1.call-done = bf16[1,128,2048]{2,1,0:T(8,128)(2,1)} async-done(((bf16[16,128,2048]{2,1,0:T(8,128)(2,1)}), bf16[1,128,2048]{2,1,0:T(8,128)(2,1)}) %reduce-scatter.3.cloned.1.call-update) | async-done | bytes 524304 | tf_op jit(solution)/shard_map/reduce_scatter | solution.py:16
  545.1 1.1 bitcast_select_fusion.1
  546.2 1.1 pad_maximum_fusion.6
  (53 shorter events, 1.2 us)
Async XLA Ops:
  7.2 18.7 %copy-start.8 = (bf16[128,4096]{1,0:T(8,128)(2,1)S(1)}, bf16[128,4096]{1,0:T(8,128)(2,1)}, u32[]{:S(2)}) copy-start(bf16[128,4096]{1,0:T(8,128)(2,1)} %param.6) | copy-start | bytes 3145732
  7.2 100.7 %all-gather.13.cloned.1.call-start = ((), (), s32[]{:S(2)}) async-start(), calls=%async_computation.6 | async-start | bytes 8912896 | tf_op jit(solution)/shard_map/all_gather | solution.py:12
  9.4 31.5 %copy-start.11 = (s32[128,8]{0,1:T(8,128)S(1)}, s32[128,8]{0,1:T(8,128)}, u32[]{:S(2)}) copy-start(s32[128,8]{0,1:T(8,128)} %param.8) | copy-start | bytes 12292
  9.4 65.1 %copy-start.12 = (bf16[128,8]{0,1:T(8,128)(2,1)S(1)}, bf16[128,8]{0,1:T(8,128)(2,1)}, u32[]{:S(2)}) copy-start(bf16[128,8]{0,1:T(8,128)(2,1)} %param.9) | copy-start | bytes 6148
  9.4 14.9 %collective-permute-start.1 = (bf16[128,2048]{1,0:T(8,128)(2,1)S(1)}, bf16[128,2048]{1,0:T(8,128)(2,1)S(1)}, u32[]{:S(2)}, u32[]{:S(2)}) collective-permute-start(bf16[128,2048]{1,0:T(8,128)(2,1)S(1)} %get-tuple-element.28), channel_id=1, source_target_pairs={{0,1},{1,0},{2,3},{3,2},{4,5},{5,4},{6,7},{7,6},{8,9},{9,8},{10,11... | collective-permute-start | bytes 1572872 | tf_op jit(solution)/shard_map/ppermute | solution.py:39
  24.3 0.8 copy-start.10
  25.1 153.5 %all-gather.11.cloned.1.call-start = ((), (), s32[]{:S(2)}) async-start(), calls=%async_computation.5 | async-start | bytes 8912896 | tf_op jit(solution)/shard_map/all_gather | solution.py:12
  25.8 234.5 %all-gather.15.cloned.1.call-start = ((), (), s32[]{:S(2)}) async-start(), calls=%async_computation.7 | async-start | bytes 8912896 | tf_op jit(solution)/shard_map/all_gather | solution.py:12
  26.8 302.4 %all-gather.17.cloned.1.call-start = ((), (), s32[]{:S(2)}) async-start(), calls=%async_computation.8 | async-start | bytes 8912896 | tf_op jit(solution)/shard_map/all_gather | solution.py:12
  26.8 13.2 %collective-permute-start.7 = (bf16[128,2048]{1,0:T(8,128)(2,1)S(1)}, bf16[128,2048]{1,0:T(8,128)(2,1)S(1)}, u32[]{:S(2)}, u32[]{:S(2)}) collective-permute-start(bf16[128,2048]{1,0:T(8,128)(2,1)S(1)} %get-tuple-element.23), channel_id=1, source_target_pairs={{0,1},{1,0},{2,3},{3,2},{4,5},{5,4},{6,7},{7,6},{8,9},{9,8},{10,11... | collective-permute-start | bytes 1572872 | tf_op jit(solution)/shard_map/ppermute | solution.py:40
  40.0 0.8 copy-start.9
  40.8 395.8 %reduce-scatter.5.cloned.1.call-start = ((), (), s32[]{:S(2)}) async-start(), calls=%async_computation.4 | async-start | bytes 8912896 | tf_op jit(solution)/shard_map/reduce_scatter | solution.py:16
  73.0 34.6 %collective-permute-start = (s32[16,128,8]{1,2,0:T(8,128)S(1)}, s32[16,128,8]{1,2,0:T(8,128)S(1)}, u32[]{:S(2)}, u32[]{:S(2)}) collective-permute-start(s32[16,128,8]{1,2,0:T(8,128)S(1)} %bitcast.57), channel_id=1, source_target_pairs={{0,1},{1,0},{2,3},{3,2},{4,5},{5,4},{6,7},{7,6},{8,9},{9,8},{10,11... | collective-permute-start | bytes 196616 | tf_op jit(solution)/shard_map/ppermute | solution.py:46
  103.7 3.9 collective-permute-start.3
  119.0 64.4 %collective-permute-start.2 = (bf16[768,768]{0,1:T(8,128)(2,1)}, bf16[768,768]{0,1:T(8,128)(2,1)}, u32[]{:S(2)}, u32[]{:S(2)}) collective-permute-start(bf16[768,768]{0,1:T(8,128)(2,1)} %get-tuple-element.29), channel_id=1, source_target_pairs={{0,1},{1,0},{2,3},{3,2},{4,5},{5,4},{6,7},{7,6},{8,9},{9,8},{10,11... | collective-permute-start | bytes 3538952 | tf_op jit(solution)/shard_map/ppermute | solution.py:84
  124.1 76.4 %collective-permute-start.5 = (bf16[768,1536]{0,1:T(8,128)(2,1)}, bf16[768,1536]{0,1:T(8,128)(2,1)}, u32[]{:S(2)}, u32[]{:S(2)}) collective-permute-start(bf16[768,1536]{0,1:T(8,128)(2,1)} %bitcast.51), channel_id=1, source_target_pairs={{0,1},{1,0},{2,3},{3,2},{4,5},{5,4},{6,7},{7,6},{8,9},{9,8},{10,11... | collective-permute-start | bytes 7077896 | tf_op jit(solution)/shard_map/ppermute | solution.py:42
  178.6 4.8 copy-start.3
  183.3 8.5 %copy-start = (bf16[16,48,2048]{2,1,0:T(8,128)(2,1)}, bf16[16,48,2048]{2,1,0:T(8,128)(2,1)S(1)}, u32[]{:S(2)}) copy-start(bf16[16,48,2048]{2,1,0:T(8,128)(2,1)S(1)} %convolution_convert_fusion.5) | copy-start | bytes 9437188
  198.9 28.4 %collective-permute-start.4 = (bf16[768,768]{0,1:T(8,128)(2,1)}, bf16[768,768]{0,1:T(8,128)(2,1)}, u32[]{:S(2)}, u32[]{:S(2)}) collective-permute-start(bf16[768,768]{0,1:T(8,128)(2,1)} %get-tuple-element.22), channel_id=1, source_target_pairs={{0,1},{1,0},{2,3},{3,2},{4,5},{5,4},{6,7},{7,6},{8,9},{9,8},{10,11... | collective-permute-start | bytes 3538952 | tf_op jit(solution)/shard_map/ppermute | solution.py:85
  231.4 9.4 %copy-start.4 = (bf16[768,768]{0,1:T(8,128)(2,1)}, bf16[768,768]{0,1:T(8,128)(2,1)S(1)}, u32[]{:S(2)}) copy-start(bf16[768,768]{0,1:T(8,128)(2,1)S(1)} %get-tuple-element.20) | copy-start | bytes 3538948
  231.4 9.4 %copy-start.5 = (bf16[768,768]{0,1:T(8,128)(2,1)}, bf16[768,768]{0,1:T(8,128)(2,1)S(1)}, u32[]{:S(2)}) copy-start(bf16[768,768]{0,1:T(8,128)(2,1)S(1)} %get-tuple-element.21) | copy-start | bytes 3538948
  246.6 298.5 %reduce-scatter.3.cloned.1.call-start = ((), (), s32[]{:S(2)}) async-start(), calls=%async_computation.3 | async-start | bytes 8912896 | tf_op jit(solution)/shard_map/reduce_scatter | solution.py:16
  336.2 25.5 %all-to-all-start = ((bf16[16,1,128]{2,1,0:T(2,128)(2,1)}), bf16[16,1,128]{2,1,0:T(2,128)(2,1)S(1)}, u32[]{:S(2)}, u32[]{:S(2)}) async-start(bf16[16,1,128]{2,1,0:T(2,128)(2,1)} %copy.14), calls=%async_computation.2 | async-start | bytes 16384 | tf_op jit(solution)/shard_map/all_to_all | solution.py:136
  345.9 6.7 %copy-start.2 = (bf16[16,48,2048]{2,1,0:T(8,128)(2,1)S(1)}, bf16[16,48,2048]{2,1,0:T(8,128)(2,1)}, u32[]{:S(2)}) copy-start(bf16[16,48,2048]{2,1,0:T(8,128)(2,1)} %convolution_convert_fusion.3) | copy-start | bytes 9437188
  345.9 6.7 %copy-start.6 = (bf16[768,768]{0,1:T(8,128)(2,1)S(1)}, bf16[768,768]{0,1:T(8,128)(2,1)}, u32[]{:S(2)}) copy-start(bf16[768,768]{0,1:T(8,128)(2,1)} %get-tuple-element.18) | copy-start | bytes 3538948
  346.0 6.7 %copy-start.7 = (bf16[768,768]{0,1:T(8,128)(2,1)S(1)}, bf16[768,768]{0,1:T(8,128)(2,1)}, u32[]{:S(2)}) copy-start(bf16[768,768]{0,1:T(8,128)(2,1)} %get-tuple-element.19) | copy-start | bytes 3538948
  352.7 9.6 %copy-start.1 = (bf16[16,48,2048]{2,1,0:T(8,128)(2,1)S(1)}, bf16[16,48,2048]{2,1,0:T(8,128)(2,1)}, u32[]{:S(2)}) copy-start(bf16[16,48,2048]{2,1,0:T(8,128)(2,1)} %convolution_convert_fusion.2) | copy-start | bytes 9437188
  436.7 108.4 %collective-permute-start.6 = (bf16[128,2048]{1,0:T(8,128)(2,1)}, bf16[128,2048]{1,0:T(8,128)(2,1)S(1)}, u32[]{:S(2)}, u32[]{:S(2)}) collective-permute-start(bf16[128,2048]{1,0:T(8,128)(2,1)} %bitcast.65), channel_id=1, source_target_pairs={{0,1},{1,0},{2,3},{3,2},{4,5},{5,4},{6,7},{7,6},{8,9},{9,8},{10,11... | collective-permute-start | bytes 1572872 | tf_op jit(solution)/shard_map/ppermute | solution.py:131
Sparse Core Ops, SparseCore 0:
  25.2 77.1 all-gather.12
  105.2 73.3 all-gather.10
  180.8 73.1 all-gather.14
  256.0 73.1 all-gather.16
  333.7 102.9 reduce-scatter.4
  440.6 104.4 reduce-scatter.2

commit v2 on v1

v2 whole, which is shorter than its diff:
```python
import jax
import jax.numpy as jnp
from jax import lax
from jax.experimental import pallas as pl
from jax.experimental.pallas import tpu as pltpu
from jax.sharding import PartitionSpec as P

PLANE = ("ctx", "tp")
F32 = jnp.float32
BF16 = jnp.bfloat16


def outer_kernel(a0, a1, g0, g1, u0, u1, s0, s1, out):
    def outer(rows, cols):
        return lax.dot_general(
            rows[...], cols[...], (((0,), (0,)), ((), ())), preferred_element_type=F32
        )

    wide = u0.shape[1]
    out[:, :wide] = (outer(a0, u0) + outer(a1, u1)).astype(BF16)
    out[:, wide:] = (outer(g0, s0) + outer(g1, s1)).astype(BF16)


def weight_outer(acts, grads, gate_up, scaled):
    slots, features = acts[0].shape
    wide, narrow = gate_up[0].shape[1], scaled[0].shape[1]
    tile = 256
    rows = pl.BlockSpec((slots, tile), lambda i: (0, i))
    whole = [pl.BlockSpec((slots, n), lambda i: (0, 0)) for n in (wide, wide, narrow, narrow)]
    return pl.pallas_call(
        outer_kernel,
        grid=(features // tile,),
        in_specs=[rows] * 4 + whole,
        out_specs=pl.BlockSpec((tile, wide + narrow), lambda i: (i, 0)),
        out_shape=jax.ShapeDtypeStruct((features, wide + narrow), BF16),
        compiler_params=pltpu.CompilerParams(vmem_limit_bytes=40 * 2**20),
        cost_estimate=pl.CostEstimate(
            flops=4 * slots * features * (wide + narrow),
            bytes_accessed=2 * (features * (4 * slots + wide + narrow) + 2 * slots * (wide + narrow)),
            transcendentals=0,
        ),
    )(*acts, *grads, *gate_up, *scaled)


def body(activations, out_grad, routes, gate_probs, saved_pre, expert_weights):
    tokens, width = activations.shape
    top_k = routes.shape[1]
    ctx_size = lax.axis_size("ctx")
    nz = lax.axis_size("tp")
    nx = ctx_size // 2
    sources = ctx_size * nz
    replica = lax.axis_index("dp")
    ctx_at = lax.axis_index("ctx")
    z_at = lax.axis_index("tp")
    x_at, core_at = ctx_at // 2, ctx_at % 2
    slots = saved_pre.shape[2]
    cap = slots // sources
    hidden = saved_pre.shape[3] // 2
    half = width // 2
    near = nx * nz

    def swap_dp(v):
        return lax.ppermute(v, "dp", [(0, 1), (1, 0)])

    def swap_core(v):
        return lax.ppermute(v, "ctx", [(i, i ^ 1) for i in range(ctx_size)])

    def move_x(v, by):
        pairs = [(i, (i // 2 + by) % nx * 2 + i % 2) for i in range(ctx_size)]
        return lax.ppermute(v, "ctx", pairs)

    def move_z(v, by):
        return lax.ppermute(v, "tp", [(i, (i + by) % nz) for i in range(nz)])

    def regroup(v):
        low, high = v[:, :half], v[:, half:]
        keep = jnp.where(replica == 0, low, high)
        other = swap_dp(jnp.where(replica == 0, high, low))
        return jnp.stack([keep, other])

    def gather_z(v):
        blocks = [v]
        for _ in range(1, nz):
            blocks.append(move_z(blocks[-1], 1))
        return blocks

    def permuted(rows_from, v):
        onehot = (rows_from[:, None] == jnp.arange(sources)[None, :]).astype(BF16)
        flat = v.reshape(sources, -1)
        moved = jnp.dot(onehot, flat, preferred_element_type=F32).astype(BF16)
        return moved.reshape(v.shape)

    note = jnp.concatenate([routes.astype(BF16), gate_probs], axis=1)
    column_notes = gather_z(jnp.stack([note, swap_dp(note)]))
    column_notes = jnp.stack(column_notes)
    spans = [column_notes] + [move_x(column_notes, t) for t in range(1, nx)]
    near_notes = jnp.stack(spans, axis=1).reshape(near, 2, tokens, 2 * top_k)
    notes = jnp.concatenate([near_notes, swap_core(near_notes)])

    order = jnp.arange(2 * near)
    src_core = jnp.bitwise_xor(order // near, core_at)
    src_z = (z_at - order // nx % nz) % nz
    src_x = (x_at - order % nx) % nx
    source_at = (src_x * 2 + src_core) * nz + src_z
    routes_at = notes[..., :top_k].astype(jnp.int32)
    probs_at = notes[..., top_k:].astype(F32)
    earlier = (
        lax.broadcasted_iota(jnp.int32, (tokens, tokens), 0)
        < lax.broadcasted_iota(jnp.int32, (tokens, tokens), 1)
    ).astype(BF16)

    def select(r, p, which):
        hit = r == which
        named = jnp.any(hit, axis=-1)
        prob = jnp.sum(jnp.where(hit, p, 0.0), axis=-1)
        rank = jnp.dot(named.astype(BF16), earlier, preferred_element_type=F32)
        place = lax.broadcasted_iota(jnp.int32, rank.shape[:2] + (cap, tokens), 2)
        chosen = named[:, :, None] & (rank.astype(jnp.int32)[:, :, None] == place)
        column = jnp.sum(jnp.where(chosen, prob[:, :, None], 0.0), axis=-1)
        return chosen, column

    mine = (x_at * 2 + core_at) * nz + z_at
    chosen_mine, column = select(routes_at, probs_at, mine)
    column_routes = column_notes[..., :top_k].astype(jnp.int32)
    column_probs = column_notes[..., top_k:].astype(F32)
    pick = []
    for t in range(nx):
        for cr in range(2):
            expert = ((x_at + t) % nx * 2 + jnp.bitwise_xor(core_at, cr)) * nz + z_at
            pick.append(select(column_routes, column_probs, expert)[0])
    pick = jnp.concatenate(pick, axis=2).astype(BF16)
    columns = column.reshape(2, slots, 1)

    from_slot = jnp.repeat(source_at, cap) * cap + jnp.tile(jnp.arange(cap), sources)
    moves = (from_slot[:, None] == lax.broadcasted_iota(jnp.int32, (slots, slots), 1)).astype(BF16)
    pre_own = jnp.dot(moves, saved_pre[0, 0], preferred_element_type=F32).astype(BF16)
    pre_own = pre_own.reshape(sources, cap, 2 * hidden)
    pre = jnp.stack([pre_own, swap_dp(pre_own)], axis=1).reshape(2, slots, 2 * hidden)

    weights = expert_weights[0]
    down_part = weights[:, 2 * hidden :]
    gate_up_part = weights[:, : 2 * hidden]

    def pack(blocks):
        kept, sent = [], []
        for h in range(nz):
            packed = jnp.einsum(
                "rpt,rtd->rpd", pick[h], blocks[h], preferred_element_type=F32
            ).astype(BF16).reshape(2, nx, 2, cap, half)
            for t in range(nx):
                rows = packed[:, t] if t == 0 else move_x(packed[:, t], t)
                kept.append(rows[:, 0])
                sent.append(rows[:, 1])
        return [
            jnp.stack(kept).reshape(slots, half),
            swap_core(jnp.stack(sent).reshape(slots, half)),
        ]

    def swap_replicas(v):
        flipped = v.reshape(near, 2, cap, v.shape[-1])[:, ::-1].reshape(v.shape)
        return swap_dp(flipped)

    grads = regroup(out_grad)
    acts = regroup(activations)
    grad_blocks = gather_z(grads)
    acts, grad_blocks[-1] = lax.optimization_barrier((acts, grad_blocks[-1]))
    act_blocks = gather_z(acts)
    grad_rows = pack(grad_blocks)

    gate_up, scaled, token_probs = [], [], []
    for i in range(2):
        part = jnp.dot(grad_rows[i], down_part, preferred_element_type=F32)
        down_grad = part + swap_replicas(part.astype(BF16)).astype(F32)
        gate = pre[i, :, :hidden].astype(F32)
        up = pre[i, :, hidden:].astype(F32)
        sig = jax.nn.sigmoid(gate)
        act = gate * sig
        hidden_act = act * up
        slot_prob = jnp.sum(hidden_act * down_grad, axis=1).astype(BF16).astype(F32)
        slot_prob = slot_prob.reshape(near, 2, cap)[:, 0, :, None]
        own = chosen_mine[i * near : (i + 1) * near, 0]
        token_probs.append(jnp.sum(jnp.where(own, slot_prob, 0.0), axis=1))
        dh = columns[i] * down_grad
        gate_up.append(
            jnp.concatenate(
                [dh * up * sig * (1.0 + gate * (1.0 - sig)), dh * act], axis=1
            ).astype(BF16)
        )
        scaled.append((columns[i] * hidden_act).astype(BF16))

    def row_grad(i):
        return lax.dot_general(
            gate_up[i], gate_up_part, (((1,), (1,)), ((), ())), preferred_element_type=F32
        ).astype(BF16)

    far_rows = swap_core(row_grad(1)).reshape(near, 2, cap, half)
    near_rows = row_grad(0).reshape(near, 2, cap, half)

    total = None
    for h in range(nz - 1, -1, -1):
        parts = []
        for t in range(nx):
            both = jnp.stack([near_rows[h * nx + t], far_rows[h * nx + t]], axis=1)
            parts.append(both if t == 0 else move_x(both, -t))
        spread = jnp.einsum(
            "rpt,rpd->rtd",
            pick[h],
            jnp.stack(parts, axis=1).reshape(2, 2 * nx * cap, half),
            preferred_element_type=F32,
        )
        total = spread if total is None else spread + move_z(total.astype(BF16), -1).astype(F32)
    total = total.astype(BF16)
    kept, back_half = total[0], swap_dp(total[1])
    input_grad = jnp.concatenate(
        [jnp.where(replica == 0, kept, back_half), jnp.where(replica == 0, back_half, kept)], axis=1
    )

    act_rows = pack(act_blocks)

    weight_grad = weight_outer(act_rows, grad_rows, gate_up, scaled)[None]

    source = jnp.arange(sources)
    s_ctx, s_z = source // nz, source % nz
    place_of = (
        jnp.bitwise_xor(s_ctx % 2, core_at) * near
        + (z_at - s_z) % nz * nx
        + (x_at - s_ctx // 2) % nx
    )
    outgoing = permuted(place_of, jnp.concatenate(token_probs).astype(BF16))
    back = lax.all_to_all(outgoing, PLANE, split_axis=0, concat_axis=0, tiled=True)
    experts = lax.broadcasted_iota(jnp.int32, (sources, tokens, top_k), 0)
    prob_grad = jnp.sum(
        jnp.where(routes[None] == experts, back[:, :, None].astype(F32), 0.0), axis=0
    ).astype(BF16)
    return (input_grad, prob_grad, weight_grad)


def solution(mesh):
    placed = (
        P(("ctx", "tp", "dp"), None),
        P(("ctx", "tp", "dp"), None),
        P(("ctx", "tp", "dp"), None),
        P(("ctx", "tp", "dp"), None),
        P(("ctx", "tp"), "dp", None, None),
        P(("ctx", "tp"), "dp", None),
    )
    return jax.shard_map(
        body,
        mesh=mesh,
        in_specs=placed,
        out_specs=(
            P(("ctx", "tp", "dp"), None),
            P(("ctx", "tp", "dp"), None),
            P(("ctx", "tp"), "dp", None),
        ),
        check_vma=False,
    )
```

time: 555 us -> 407 us (0.73)
  waiting for transfers between devices: 318 us -> 218 us
  blocking collectives: 61.4 us -> 0 us
  matrix products: 99.5 us -> 45.3 us
  starting transfers between devices: 15.9 us -> 55.3 us
  Pallas kernels: 0 us -> 19.2 us
  other arithmetic: 24.8 us -> 38.6 us
  between operations: 14.3 us -> 1.5 us
  local copies, waits for them, and re-layouts: 19.8 us -> 28.9 us
    reduce_scatter x2 -> x0, waiting for transfers between devices: 149 us -> none  [scatter_plane(): return lax.psum_scatter(x, PLANE, scatter_dimension=0, tiled=False)]
    ppermute x8 -> x36, waiting for transfers between devices: 53.2 us -> 202 us  [the longest x13 72.1 us: move_x(): return lax.ppermute(v, 'ctx', pairs)]
    all_gather x4 -> x0, waiting for transfers between devices: 115 us -> none  [gather_plane(): return lax.all_gather(x, PLANE, axis=0, tiled=False)]
    all_gather x2 -> x0, blocking collectives: 61.4 us -> none  [the longest x1 32.1 us: body(): routes_own = lax.all_gather(routes, PLANE, axis=0, tiled=False)]
    dot_general x14 -> x18, matrix products: 99.2 us -> 44.6 us  [the longest x2 13.6 us: body(): part = jnp.dot(grad_rows[i], down_part, preferred_element_type=F32)]
    ppermute x8 -> x36, starting transfers between devices: 11.9 us -> 51.5 us  [the longest x12 23.3 us: move_z(): return lax.ppermute(v, 'tp', [(i, (i + by) % nz) for i in range(nz)])]
    pallas_call x0 -> x1, Pallas kernels: none -> 19.2 us  [weight_outer(): pl.pallas_call(outer_kernel, grid=(features // tile,), in_specs=[rows] *...]
    all_to_all x1, waiting for transfers between devices: 0.01 us -> 15.6 us  [body(): lax.all_to_all(outgoing, PLANE, split_axis=0, concat_axis=0, tiled=True)]
  transfers between devices with their start and end apart: 15 -> 37, of which waited for: 8 -> 23; matrix products, arithmetic and copies ran while one was open for 25% -> 26% of each run, Pallas kernels for 0% -> 5%
where the time goes in v2:
time: 407 us; the launch traced here: 406 us
  waiting for transfers between devices  218 us (54%)
  starting transfers between devices  55.3 us (14%)
  matrix products  45.3 us (11%)
  other arithmetic  38.6 us (9%)
  local copies, waits for them, and re-layouts  28.9 us (7%)
  Pallas kernels  19.2 us (5%)
    ppermute x13, waiting for transfers between devices, move_x(): return lax.ppermute(v, 'ctx', pairs)  72.1 us
    ppermute x7, waiting for transfers between devices, swap_dp(): return lax.ppermute(v, 'dp', [(0, 1), (1, 0)])  68.8 us
    ppermute x12, waiting for transfers between devices, move_z(): return lax.ppermute(v, 'tp', [(i, (i + by) % nz) for i in range(nz)])  59.9 us
    ppermute x12, starting transfers between devices, move_z(): return lax.ppermute(v, 'tp', [(i, (i + by) % nz) for i in range(nz)])  23.3 us
    pallas_call x1, Pallas kernels, weight_outer(): pl.pallas_call(outer_kernel, grid=(features // tile,), in_specs=[rows] *...  19.2 us
    ppermute x13, starting transfers between devices, move_x(): return lax.ppermute(v, 'ctx', pairs)  17 us
    unnamed x92, local copies, waits for them, and re-layouts  16.1 us
    all_to_all x1, waiting for transfers between devices, body(): lax.all_to_all(outgoing, PLANE, split_axis=0, concat_axis=0, tiled=True)  15.6 us
  transfers between devices with their start and end apart: 37, of which 23 were waited for; matrix products, arithmetic and copies ran while one was open for 26% of the time, Pallas kernels for 5%

profile of v2, /device:TPU:0, one launch (start us, length us, event | category | flops | bytes accessed | tf_op | source)
XLA Modules:
  0.0 406.4 jit_solution(14651829737307900102)
XLA Ops:
  2.2 3.0 collective-permute-start
  6.7 2.1 collective-permute-start.1
  8.8 3.4 convolution_convert_fusion
  15.4 2.1 select_bitcast_fusion.1
  19.5 2.2 select_bitcast_fusion
  31.7 46.3 %collective-permute-done.6 = bf16[128,2048]{1,0:T(8,128)(2,1)} collective-permute-done((bf16[128,2048]{1,0:T(8,128)(2,1)}, bf16[128,2048]{1,0:T(8,128)(2,1)}, u32[]{:S(2)}, u32[]{:S(2)}) %collective-permute-start.6) | collective-permute-done | bytes 524320 | tf_op jit(solution)/shard_map/ppermute | solution.py:63
  86.6 2.1 pad_maximum_fusion.8
  88.7 13.8 %collective-permute-done.8 = bf16[2,128,2048]{2,1,0:T(8,128)(2,1)S(1)} collective-permute-done((bf16[2,128,2048]{2,1,0:T(8,128)(2,1)S(1)}, bf16[2,128,2048]{2,1,0:T(8,128)(2,1)S(1)}, u32[]{:S(2)}, u32[]{:S(2)}) %collective-permute-start.8) | collective-permute-done | bytes 1048608 | tf_op jit(solution)/shard_map/ppermute | solution.py:73
  107.3 9.5 %collective-permute-done.9 = bf16[2,2,48,2048]{3,2,0,1:T(8,128)(2,1)S(1)} collective-permute-done((bf16[2,2,48,2048]{3,2,0,1:T(8,128)(2,1)S(1)}, bf16[2,2,48,2048]{3,2,0,1:T(8,128)(2,1)S(1)}, u32[]{:S(2)}, u32[]{:S(2)}) %collective-permute-start.9) | collective-permute-done | bytes 786464 | tf_op jit(solution)/shard_map/ppermute | solution.py:70
  117.6 2.1 pad_maximum_fusion
  119.7 8.3 %collective-permute-done.10 = bf16[2,128,2048]{2,1,0:T(8,128)(2,1)S(1)} collective-permute-done((bf16[2,128,2048]{2,1,0:T(8,128)(2,1)S(1)}, bf16[2,128,2048]{2,1,0:T(8,128)(2,1)S(1)}, u32[]{:S(2)}, u32[]{:S(2)}) %collective-permute-start.10) | collective-permute-done | bytes 1048608 | tf_op jit(solution)/shard_map/ppermute | solution.py:73
  129.3 1.8 multiply_convert_fusion.1.s0
  131.9 9.0 %collective-permute-done.11 = bf16[2,2,48,2048]{3,2,0,1:T(8,128)(2,1)S(1)} collective-permute-done((bf16[2,2,48,2048]{3,2,0,1:T(8,128)(2,1)S(1)}, bf16[2,2,48,2048]{3,2,0,1:T(8,128)(2,1)S(1)}, u32[]{:S(2)}, u32[]{:S(2)}) %collective-permute-start.11) | collective-permute-done | bytes 786464 | tf_op jit(solution)/shard_map/ppermute | solution.py:70
  141.7 8.3 %collective-permute-done.13 = bf16[2,128,2048]{2,1,0:T(8,128)(2,1)S(1)} collective-permute-done((bf16[2,128,2048]{2,1,0:T(8,128)(2,1)S(1)}, bf16[2,128,2048]{2,1,0:T(8,128)(2,1)S(1)}, u32[]{:S(2)}, u32[]{:S(2)}) %collective-permute-start.13) | collective-permute-done | bytes 1048608 | tf_op jit(solution)/shard_map/ppermute | solution.py:73
  150.1 1.8 convolution_convert_fusion.4
  153.3 1.7 collective-permute-start.14
  156.1 9.3 %collective-permute-done.14 = bf16[2,2,48,2048]{3,2,0,1:T(8,128)(2,1)S(1)} collective-permute-done((bf16[2,2,48,2048]{3,2,0,1:T(8,128)(2,1)S(1)}, bf16[2,2,48,2048]{3,2,0,1:T(8,128)(2,1)S(1)}, u32[]{:S(2)}, u32[]{:S(2)}) %collective-permute-start.14) | collective-permute-done | bytes 786464 | tf_op jit(solution)/shard_map/ppermute | solution.py:70
  168.3 1.6 collective-permute-start.28
  169.9 6.3 %fusion.125 = (bf16[768,768]{1,0:T(8,128)(2,1)}, f32[768,768]{1,0:T(8,128)}) fusion(bf16[768,2048]{1,0:T(8,128)(2,1)S(1)} %bitcast.424, bf16[2048,2304]{1,0:T(8,128)(2,1)} %bitcast.434), kind=kOutput, calls=%fused_computation.298 | convolution fusion | flops 2416508928 | bytes 9830400 | tf_op jit(solution)/shard_map/dot_general | solution.py:172
  176.2 2.4 rev.6
  180.1 1.8 convolution_convert_fusion.3
  182.6 6.4 %collective-permute-done.28 = bf16[2,2,48,2048]{3,2,0,1:T(8,128)(2,1)} collective-permute-done((bf16[2,2,48,2048]{3,2,0,1:T(8,128)(2,1)}, bf16[2,2,48,2048]{3,2,0,1:T(8,128)(2,1)}, u32[]{:S(2)}, u32[]{:S(2)}) %collective-permute-start.28) | collective-permute-done | bytes 786464 | tf_op jit(solution)/shard_map/ppermute | solution.py:70
  188.9 1.9 fusion.38
  191.0 2.5 collective-permute-start.31
  194.3 10.7 %collective-permute-done.30 = bf16[2,2,48,2048]{3,2,0,1:T(8,128)(2,1)S(1)} collective-permute-done((bf16[2,2,48,2048]{3,2,0,1:T(8,128)(2,1)S(1)}, bf16[2,2,48,2048]{3,2,0,1:T(8,128)(2,1)S(1)}, u32[]{:S(2)}, u32[]{:S(2)}) %collective-permute-start.30) | collective-permute-done | bytes 786464 | tf_op jit(solution)/shard_map/ppermute | solution.py:70
  205.9 7.3 %fusion.126 = (bf16[768,768]{1,0:T(8,128)(2,1)}, f32[768,768]{1,0:T(8,128)}) fusion(bf16[768,2048]{1,0:T(8,128)(2,1)} %collective-permute-done.17.g1, bf16[2048,2304]{1,0:T(8,128)(2,1)} %bitcast.435), kind=kOutput, calls=%fused_computation.299 | convolution fusion | flops 2416508928 | bytes 9830400 | tf_op jit(solution)/shard_map/dot_general | solution.py:172
  213.2 2.5 rev.7
  217.4 1.9 convolution_convert_fusion.2
  223.2 20.1 %collective-permute-done.18 = bf16[768,768]{1,0:T(8,128)(2,1)S(1)} collective-permute-done((bf16[768,768]{1,0:T(8,128)(2,1)}, bf16[768,768]{1,0:T(8,128)(2,1)S(1)}, u32[]{:S(2)}, u32[]{:S(2)}) %collective-permute-start.18) | collective-permute-done | bytes 1179680 | tf_op jit(solution)/shard_map/ppermute | solution.py:63
  243.3 5.4 %multiply_reduce_fusion.1 = (bf16[768]{0:T(1024)(128)(2,1)S(1)}, bf16[768]{0:T(1024)(128)(2,1)S(1)}, bf16[768,768]{1,0:T(8,128)(2,1)S(1)}, bf16[768,768]{1,0:T(8...) fusion(bf16[2,768,1536]{2,1,0:T(8,128)(2,1)S(1)} %bitcast.371, ...), kind=kLoop, calls=%fused_computation.51 | loop fusion | flops 25950720 | bytes 17703936 | tf_op jit(solution)/shard_map/reduce_sum | solution.py:179
  248.8 5.3 %fusion.7 = bf16[768,2048]{1,0:T(8,128)(2,1)S(1)} fusion(bf16[2048,2304]{1,0:T(8,128)(2,1)S(1)} %bitcast.438, bf16[768,768]{1,0:T(8,128)(2,1)S(1)} %get-tuple-element.21, bf16[768,768]{1,0:T(8,128)(2,1)S(1)} %get-tuple-element.22), kind=kOutput, calls=%fused_computation.13 | convolution fusion | flops 4838129664 | bytes 11796480 | tf_op jit(solution)/shard_map/dot_general | solution.py:192
  256.8 1.7 collective-permute-start.34
  259.6 5.3 %fusion.4 = bf16[768,2048]{1,0:T(8,128)(2,1)S(1)} fusion(bf16[2048,2304]{1,0:T(8,128)(2,1)S(1)} %bitcast.439, bf16[768,768]{1,0:T(8,128)(2,1)S(1)} %get-tuple-element.23, bf16[768,768]{1,0:T(8,128)(2,1)S(1)} %get-tuple-element.24), kind=kOutput, calls=%fused_computation.12 | convolution fusion | flops 4838129664 | bytes 11796480 | tf_op jit(solution)/shard_map/dot_general | solution.py:192
  269.3 8.0 %collective-permute-done.34 = bf16[2,2,48,2048]{3,2,0,1:T(8,128)(2,1)S(1)} collective-permute-done((bf16[2,2,48,2048]{3,2,0,1:T(8,128)(2,1)S(1)}, bf16[2,2,48,2048]{3,2,0,1:T(8,128)(2,1)S(1)}, u32[]{:S(2)}, u32[]{:S(2)}) %collective-permute-start.34) | collective-permute-done | bytes 786464 | tf_op jit(solution)/shard_map/ppermute | solution.py:70
  279.5 1.7 collective-permute-start.22
  282.4 11.8 %collective-permute-done.23 = bf16[2,2,48,2048]{3,2,0,1:T(8,128)(2,1)} collective-permute-done((bf16[2,2,48,2048]{3,2,0,1:T(8,128)(2,1)}, bf16[2,2,48,2048]{3,2,0,1:T(8,128)(2,1)}, u32[]{:S(2)}, u32[]{:S(2)}) %collective-permute-start.23) | collective-permute-done | bytes 786464 | tf_op jit(solution)/shard_map/ppermute | solution.py:70
  297.0 4.0 collective-permute-start.24
  305.1 5.8 %collective-permute-done.22 = bf16[2,2,48,2048]{3,2,0,1:T(8,128)(2,1)S(1)} collective-permute-done((bf16[2,2,48,2048]{3,2,0,1:T(8,128)(2,1)S(1)}, bf16[2,2,48,2048]{3,2,0,1:T(8,128)(2,1)S(1)}, u32[]{:S(2)}, u32[]{:S(2)}) %collective-permute-start.22) | collective-permute-done | bytes 786464 | tf_op jit(solution)/shard_map/ppermute | solution.py:70
  311.3 11.6 %collective-permute-done.24 = bf16[2,128,2048]{2,1,0:T(8,128)(2,1)S(1)} collective-permute-done((bf16[2,128,2048]{2,1,0:T(8,128)(2,1)S(1)}, bf16[2,128,2048]{2,1,0:T(8,128)(2,1)S(1)}, u32[]{:S(2)}, u32[]{:S(2)}) %collective-permute-start.24) | collective-permute-done | bytes 1048608 | tf_op jit(solution)/shard_map/ppermute | solution.py:73
  324.3 4.3 %collective-permute-start.25 = (bf16[2,128,2048]{2,1,0:T(8,128)(2,1)}, bf16[2,128,2048]{2,1,0:T(8,128)(2,1)}, u32[]{:S(2)}, u32[]{:S(2)}) collective-permute-start(bf16[2,128,2048]{2,1,0:T(8,128)(2,1)} %add_convert_fusion.2), channel_id=1, source_target_pairs={{0,6},{2,0},{4,2},{6,4},{1,7},{3,1},{5,3},{7,5},{8,14},{10,8},{12,... | collective-permute-start | bytes 3145736 | tf_op jit(solution)/shard_map/ppermute | solution.py:73
  328.7 2.1 pad_maximum_fusion.10
  335.0 14.9 %collective-permute-done.25 = bf16[2,128,2048]{2,1,0:T(8,128)(2,1)} collective-permute-done((bf16[2,128,2048]{2,1,0:T(8,128)(2,1)}, bf16[2,128,2048]{2,1,0:T(8,128)(2,1)}, u32[]{:S(2)}, u32[]{:S(2)}) %collective-permute-start.25) | collective-permute-done | bytes 1048608 | tf_op jit(solution)/shard_map/ppermute | solution.py:73
  349.9 2.8 add_convert_fusion.1
  352.7 4.3 %collective-permute-start.26 = (bf16[2,128,2048]{2,1,0:T(8,128)(2,1)}, bf16[2,128,2048]{2,1,0:T(8,128)(2,1)}, u32[]{:S(2)}, u32[]{:S(2)}) collective-permute-start(bf16[2,128,2048]{2,1,0:T(8,128)(2,1)} %add_convert_fusion.1), channel_id=1, source_target_pairs={{0,6},{2,0},{4,2},{6,4},{1,7},{3,1},{5,3},{7,5},{8,14},{10,8},{12,... | collective-permute-start | bytes 3145736 | tf_op jit(solution)/shard_map/ppermute | solution.py:73
  358.0 3.7 all-to-all-start
  363.4 15.6 %all-to-all-done = bf16[16,1,128]{2,1,0:T(2,128)(2,1)S(1)} async-done(((bf16[16,1,128]{2,1,0:T(2,128)(2,1)}), bf16[16,1,128]{2,1,0:T(2,128)(2,1)S(1)}, u32[]{:S(2)}, u32[]{:S(2)}) %all-to-all-start) | async-done | bytes 4128 | tf_op jit(solution)/shard_map/all_to_all | solution.py:230
  382.5 1.9 add_convert_fusion
  386.1 19.2 %shard_map.85 = bf16[2048,2304]{1,0:T(8,128)(2,1)} custom-call(bf16[768,2048]{1,0:T(8,128)(2,1)S(1)} %bitcast.367, bf16[768,2048]{1,0:T(8,128)(2,1)} %collective-permute-done.35.a1, bf16[768,2048]{1,0:T(8,128)(2,1)} %bitcast.425, bf16[768,2048]{1,0:T(8,128)(2,1)} %collective-permute-done.17.g1, bf16[768,1536]{1,0:T(8,128)(2,1)S(1)} %copy-done.2, ...), custom_call_target="tpu_custom_call" | custom-call | flops 14495514624 | bytes 29097984 | tf_op jit(solution)/shard_map/pallas_call | solution.py:30
  (219 shorter events, 83.3 us)
Async XLA Ops:
  2.2 4.6 %collective-permute-start = (bf16[128,16]{0,1:T(8,128)(2,1)S(1)}, bf16[128,16]{0,1:T(8,128)(2,1)S(1)}, u32[]{:S(2)}, u32[]{:S(2)}) collective-permute-start(bf16[128,16]{0,1:T(8,128)(2,1)S(1)} %get-tuple-element.103), channel_id=1, source_target_pairs={{0,1},{1,0},{2,3},{3,2},{4,5},{5,4},{6,7},{7,6},{8,9},{9,8},{10,11... | collective-permute-start | bytes 12296 | tf_op jit(solution)/shard_map/ppermute | solution.py:63
  6.7 7.1 %collective-permute-start.1 = (bf16[2,128,16]{1,2,0:T(8,128)(2,1)S(1)}, bf16[2,128,16]{1,2,0:T(8,128)(2,1)S(1)}, u32[]{:S(2)}, u32[]{:S(2)}) collective-permute-start(bf16[2,128,16]{1,2,0:T(8,128)(2,1)S(1)} %get-tuple-element.101), channel_id=1, source_target_pairs={{0,2},{2,4},{4,6},{6,0},{1,3},{3,5},{5,7},{7,1},{8,10},{10,12},{12... | collective-permute-start | bytes 24584 | tf_op jit(solution)/shard_map/ppermute | solution.py:73
  12.3 105.3 %collective-permute-start.16 = (bf16[16,48,1536]{2,1,0:T(8,128)(2,1)}, bf16[16,48,1536]{2,1,0:T(8,128)(2,1)S(1)}, u32[]{:S(2)}, u32[]{:S(2)}) collective-permute-start(bf16[16,48,1536]{2,1,0:T(8,128)(2,1)} %bitcast.46), channel_id=1, source_target_pairs={{0,1},{1,0},{2,3},{3,2},{4,5},{5,4},{6,7},{7,6},{8,9},{9,8},{10,11... | collective-permute-start | bytes 7077896 | tf_op jit(solution)/shard_map/ppermute | solution.py:63
  13.8 5.4 %collective-permute-start.2 = (bf16[2,128,16]{1,2,0:T(8,128)(2,1)S(1)}, bf16[2,128,16]{1,2,0:T(8,128)(2,1)S(1)}, u32[]{:S(2)}, u32[]{:S(2)}) collective-permute-start(bf16[2,128,16]{1,2,0:T(8,128)(2,1)S(1)} %collective-permute-done.1), channel_id=1, source_target_pairs={{0,2},{2,4},{4,6},{6,0},{1,3},{3,5},{5,7},{7,1},{8,10},{10,12},{12... | collective-permute-start | bytes 24584 | tf_op jit(solution)/shard_map/ppermute | solution.py:73
  17.4 60.6 %collective-permute-start.6 = (bf16[128,2048]{1,0:T(8,128)(2,1)}, bf16[128,2048]{1,0:T(8,128)(2,1)}, u32[]{:S(2)}, u32[]{:S(2)}) collective-permute-start(bf16[128,2048]{1,0:T(8,128)(2,1)} %get-tuple-element.63), channel_id=1, source_target_pairs={{0,1},{1,0},{2,3},{3,2},{4,5},{5,4},{6,7},{7,6},{8,9},{9,8},{10,11... | collective-permute-start | bytes 1572872 | tf_op jit(solution)/shard_map/ppermute | solution.py:63
  19.2 5.4 %collective-permute-start.3 = (bf16[2,128,16]{1,2,0:T(8,128)(2,1)S(1)}, bf16[2,128,16]{1,2,0:T(8,128)(2,1)S(1)}, u32[]{:S(2)}, u32[]{:S(2)}) collective-permute-start(bf16[2,128,16]{1,2,0:T(8,128)(2,1)S(1)} %collective-permute-done.2), channel_id=1, source_target_pairs={{0,2},{2,4},{4,6},{6,0},{1,3},{3,5},{5,7},{7,1},{8,10},{10,12},{12... | collective-permute-start | bytes 24584 | tf_op jit(solution)/shard_map/ppermute | solution.py:73
  21.7 64.9 %collective-permute-start.12 = (bf16[128,2048]{1,0:T(8,128)(2,1)}, bf16[128,2048]{1,0:T(8,128)(2,1)}, u32[]{:S(2)}, u32[]{:S(2)}) collective-permute-start(bf16[128,2048]{1,0:T(8,128)(2,1)} %get-tuple-element.61), channel_id=1, source_target_pairs={{0,1},{1,0},{2,3},{3,2},{4,5},{5,4},{6,7},{7,6},{8,9},{9,8},{10,11... | collective-permute-start | bytes 1572872 | tf_op jit(solution)/shard_map/ppermute | solution.py:63
  24.7 4.0 collective-permute-start.4
  28.7 1.3 collective-permute-start.5
  28.8 188.6 %copy-start.12 = (pred[4,2,192,128]{3,2,1,0:T(32,128)(4,1)}, pred[4,2,192,128]{3,2,1,0:T(32,128)(4,1)S(1)}, u32[]{:S(2)}) copy-start(pred[4,2,192,128]{3,2,1,0:T(32,128)(4,1)S(1)} %pad_add_fusion) | copy-start | bytes 589828
  80.7 21.8 %collective-permute-start.8 = (bf16[2,128,2048]{2,1,0:T(8,128)(2,1)S(1)}, bf16[2,128,2048]{2,1,0:T(8,128)(2,1)S(1)}, u32[]{:S(2)}, u32[]{:S(2)}) collective-permute-start(bf16[2,128,2048]{2,1,0:T(8,128)(2,1)S(1)} %pad_maximum_fusion.7), channel_id=1, source_target_pairs={{0,2},{2,4},{4,6},{6,0},{1,3},{3,5},{5,7},{7,1},{8,10},{10,12},{12... | collective-permute-start | bytes 3145736 | tf_op jit(solution)/shard_map/ppermute | solution.py:73
  82.7 22.2 %collective-permute-start.7 = (bf16[2,2,48,2048]{3,2,0,1:T(8,128)(2,1)S(1)}, bf16[2,2,48,2048]{3,2,0,1:T(8,128)(2,1)S(1)}, u32[]{:S(2)}, u32[]{:S(2)}) collective-permute-start(bf16[2,2,48,2048]{3,2,0,1:T(8,128)(2,1)S(1)} %bitcast.415), channel_id=1, source_target_pairs={{0,16},{8,24},{16,0},{24,8},{1,17},{9,25},{17,1},{25,9},{2,18},{10... | collective-permute-start | bytes 2359304 | tf_op jit(solution)/shard_map/ppermute | solution.py:70
  103.3 13.5 %collective-permute-start.9 = (bf16[2,2,48,2048]{3,2,0,1:T(8,128)(2,1)S(1)}, bf16[2,2,48,2048]{3,2,0,1:T(8,128)(2,1)S(1)}, u32[]{:S(2)}, u32[]{:S(2)}) collective-permute-start(bf16[2,2,48,2048]{3,2,0,1:T(8,128)(2,1)S(1)} %bitcast.416), channel_id=1, source_target_pairs={{0,16},{8,24},{16,0},{24,8},{1,17},{9,25},{17,1},{25,9},{2,18},{10... | collective-permute-start | bytes 2359304 | tf_op jit(solution)/shard_map/ppermute | solution.py:70
  105.8 22.2 %collective-permute-start.10 = (bf16[2,128,2048]{2,1,0:T(8,128)(2,1)S(1)}, bf16[2,128,2048]{2,1,0:T(8,128)(2,1)S(1)}, u32[]{:S(2)}, u32[]{:S(2)}) collective-permute-start(bf16[2,128,2048]{2,1,0:T(8,128)(2,1)S(1)} %collective-permute-done.8), channel_id=1, source_target_pairs={{0,2},{2,4},{4,6},{6,0},{1,3},{3,5},{5,7},{7,1},{8,10},{10,12},{12... | collective-permute-start | bytes 3145736 | tf_op jit(solution)/shard_map/ppermute | solution.py:73
  128.8 12.1 %collective-permute-start.11 = (bf16[2,2,48,2048]{3,2,0,1:T(8,128)(2,1)S(1)}, bf16[2,2,48,2048]{3,2,0,1:T(8,128)(2,1)S(1)}, u32[]{:S(2)}, u32[]{:S(2)}) collective-permute-start(bf16[2,2,48,2048]{3,2,0,1:T(8,128)(2,1)S(1)} %bitcast.418), channel_id=1, source_target_pairs={{0,16},{8,24},{16,0},{24,8},{1,17},{9,25},{17,1},{25,9},{2,18},{10... | collective-permute-start | bytes 2359304 | tf_op jit(solution)/shard_map/ppermute | solution.py:70
  128.9 21.1 %collective-permute-start.13 = (bf16[2,128,2048]{2,1,0:T(8,128)(2,1)S(1)}, bf16[2,128,2048]{2,1,0:T(8,128)(2,1)S(1)}, u32[]{:S(2)}, u32[]{:S(2)}) collective-permute-start(bf16[2,128,2048]{2,1,0:T(8,128)(2,1)S(1)} %collective-permute-done.10), channel_id=1, source_target_pairs={{0,2},{2,4},{4,6},{6,0},{1,3},{3,5},{5,7},{7,1},{8,10},{10,12},{12... | collective-permute-start | bytes 3145736 | tf_op jit(solution)/shard_map/ppermute | solution.py:73
  151.9 28.2 %collective-permute-start.29 = (bf16[2,128,2048]{2,1,0:T(8,128)(2,1)}, bf16[2,128,2048]{2,1,0:T(8,128)(2,1)}, u32[]{:S(2)}, u32[]{:S(2)}) collective-permute-start(bf16[2,128,2048]{2,1,0:T(8,128)(2,1)} %pad_maximum_fusion.8), channel_id=1, source_target_pairs={{0,2},{2,4},{4,6},{6,0},{1,3},{3,5},{5,7},{7,1},{8,10},{10,12},{12... | collective-permute-start | bytes 3145736 | tf_op jit(solution)/shard_map/ppermute | solution.py:73
  153.3 12.1 %collective-permute-start.14 = (bf16[2,2,48,2048]{3,2,0,1:T(8,128)(2,1)S(1)}, bf16[2,2,48,2048]{3,2,0,1:T(8,128)(2,1)S(1)}, u32[]{:S(2)}, u32[]{:S(2)}) collective-permute-start(bf16[2,2,48,2048]{3,2,0,1:T(8,128)(2,1)S(1)} %bitcast.419), channel_id=1, source_target_pairs={{0,16},{8,24},{16,0},{24,8},{1,17},{9,25},{17,1},{25,9},{2,18},{10... | collective-permute-start | bytes 2359304 | tf_op jit(solution)/shard_map/ppermute | solution.py:70
  166.2 39.7 %collective-permute-start.17 = (bf16[768,2048]{1,0:T(8,128)(2,1)}, bf16[768,2048]{1,0:T(8,128)(2,1)}, u32[]{:S(2)}, u32[]{:S(2)}) collective-permute-start(bf16[768,2048]{1,0:T(8,128)(2,1)} %bitcast.61), channel_id=1, source_target_pairs={{0,8},{8,0},{16,24},{24,16},{1,9},{9,1},{17,25},{25,17},{2,10},{10... | collective-permute-start | bytes 9437192 | tf_op jit(solution)/shard_map/ppermute | solution.py:66
  168.3 20.7 %collective-permute-start.28 = (bf16[2,2,48,2048]{3,2,0,1:T(8,128)(2,1)}, bf16[2,2,48,2048]{3,2,0,1:T(8,128)(2,1)}, u32[]{:S(2)}, u32[]{:S(2)}) collective-permute-start(bf16[2,2,48,2048]{3,2,0,1:T(8,128)(2,1)} %bitcast.357), channel_id=1, source_target_pairs={{0,16},{8,24},{16,0},{24,8},{1,17},{9,25},{17,1},{25,9},{2,18},{10... | collective-permute-start | bytes 2359304 | tf_op jit(solution)/shard_map/ppermute | solution.py:70
  178.5 44.6 %collective-permute-start.15 = (bf16[768,768]{1,0:T(8,128)(2,1)}, bf16[768,768]{1,0:T(8,128)(2,1)}, u32[]{:S(2)}, u32[]{:S(2)}) collective-permute-start(bf16[768,768]{1,0:T(8,128)(2,1)} %bitcast.409), channel_id=1, source_target_pairs={{0,1},{1,0},{2,3},{3,2},{4,5},{5,4},{6,7},{7,6},{8,9},{9,8},{10,11... | collective-permute-start | bytes 3538952 | tf_op jit(solution)/shard_map/ppermute | solution.py:63
  182.1 22.9 %collective-permute-start.30 = (bf16[2,2,48,2048]{3,2,0,1:T(8,128)(2,1)S(1)}, bf16[2,2,48,2048]{3,2,0,1:T(8,128)(2,1)S(1)}, u32[]{:S(2)}, u32[]{:S(2)}) collective-permute-start(bf16[2,2,48,2048]{3,2,0,1:T(8,128)(2,1)S(1)} %bitcast.417), channel_id=1, source_target_pairs={{0,16},{8,24},{16,0},{24,8},{1,17},{9,25},{17,1},{25,9},{2,18},{10... | collective-permute-start | bytes 2359304 | tf_op jit(solution)/shard_map/ppermute | solution.py:70
  191.0 26.4 %collective-permute-start.31 = (bf16[2,128,2048]{2,1,0:T(8,128)(2,1)}, bf16[2,128,2048]{2,1,0:T(8,128)(2,1)}, u32[]{:S(2)}, u32[]{:S(2)}) collective-permute-start(bf16[2,128,2048]{2,1,0:T(8,128)(2,1)} %collective-permute-done.29), channel_id=1, source_target_pairs={{0,2},{2,4},{4,6},{6,0},{1,3},{3,5},{5,7},{7,1},{8,10},{10,12},{12... | collective-permute-start | bytes 3145736 | tf_op jit(solution)/shard_map/ppermute | solution.py:73
  215.6 27.6 %collective-permute-start.18 = (bf16[768,768]{1,0:T(8,128)(2,1)}, bf16[768,768]{1,0:T(8,128)(2,1)S(1)}, u32[]{:S(2)}, u32[]{:S(2)}) collective-permute-start(bf16[768,768]{1,0:T(8,128)(2,1)} %bitcast.410), channel_id=1, source_target_pairs={{0,1},{1,0},{2,3},{3,2},{4,5},{5,4},{6,7},{7,6},{8,9},{9,8},{10,11... | collective-permute-start | bytes 3538952 | tf_op jit(solution)/shard_map/ppermute | solution.py:63
  217.4 25.9 %slice-start = ((s8[4718592]{0:T(1024)(128)(4,1)}), s8[4194304]{0:T(1024)(128)(4,1)S(1)}, s32[]{:S(2)}) async-start(s8[4718592]{0:T(1024)(128)(4,1)} %bitcast.369), calls=%async_computation.1 | async-start | bytes 8388608
  219.3 24.0 %slice-start.1 = ((s8[4718592]{0:T(1024)(128)(4,1)}), s8[524288]{0:T(1024)(128)(4,1)S(1)}, s32[]{:S(2)}) async-start(s8[4718592]{0:T(1024)(128)(4,1)} %bitcast.369), calls=%async_computation.2 | async-start | bytes 1048576
  219.5 23.8 %copy-start.14 = (f32[768,768]{1,0:T(8,128)S(1)}, f32[768,768]{1,0:T(8,128)}, u32[]{:S(2)}) copy-start(f32[768,768]{1,0:T(8,128)} %get-tuple-element.105) | copy-start | bytes 7077892
  219.5 23.8 %copy-start.15 = (f32[768,768]{1,0:T(8,128)S(1)}, f32[768,768]{1,0:T(8,128)}, u32[]{:S(2)}) copy-start(f32[768,768]{1,0:T(8,128)} %get-tuple-element.107) | copy-start | bytes 7077892
  219.6 29.2 %slice-start.2 = ((s8[9437184]{0:T(1024)(128)(4,1)}), s8[4194304]{0:T(1024)(128)(4,1)S(1)}, s32[]{:S(2)}) async-start(s8[9437184]{0:T(1024)(128)(4,1)} %bitcast.436), calls=%async_computation.3 | async-start | bytes 8388608
  219.7 34.5 %collective-permute-start.32 = (bf16[2,2,48,2048]{3,2,0,1:T(8,128)(2,1)S(1)}, bf16[2,2,48,2048]{3,2,0,1:T(8,128)(2,1)S(1)}, u32[]{:S(2)}, u32[]{:S(2)}) collective-permute-start(bf16[2,2,48,2048]{3,2,0,1:T(8,128)(2,1)S(1)} %bitcast.413), channel_id=1, source_target_pairs={{0,16},{8,24},{16,0},{24,8},{1,17},{9,25},{17,1},{25,9},{2,18},{10... | collective-permute-start | bytes 2359304 | tf_op jit(solution)/shard_map/ppermute | solution.py:70
  221.3 33.9 %collective-permute-start.33 = (bf16[2,128,2048]{2,1,0:T(8,128)(2,1)}, bf16[2,128,2048]{2,1,0:T(8,128)(2,1)S(1)}, u32[]{:S(2)}, u32[]{:S(2)}) collective-permute-start(bf16[2,128,2048]{2,1,0:T(8,128)(2,1)} %collective-permute-done.31), channel_id=1, source_target_pairs={{0,2},{2,4},{4,6},{6,0},{1,3},{3,5},{5,7},{7,1},{8,10},{10,12},{12... | collective-permute-start | bytes 3145736 | tf_op jit(solution)/shard_map/ppermute | solution.py:73
  223.2 20.1 %copy-start.5 = (bf16[8,2,48,2048]{3,2,1,0:T(8,128)(2,1)}, bf16[8,2,48,2048]{3,2,1,0:T(8,128)(2,1)S(1)}, u32[]{:S(2)}) copy-start(bf16[8,2,48,2048]{3,2,1,0:T(8,128)(2,1)S(1)} %get-tuple-element.71) | copy-start | bytes 9437188
  254.2 12.2 %collective-permute-start.19 = (bf16[768,2048]{1,0:T(8,128)(2,1)S(1)}, bf16[768,2048]{1,0:T(8,128)(2,1)S(1)}, u32[]{:S(2)}, u32[]{:S(2)}) collective-permute-start(bf16[768,2048]{1,0:T(8,128)(2,1)S(1)} %fusion.7), channel_id=1, source_target_pairs={{0,8},{8,0},{16,24},{24,16},{1,9},{9,1},{17,25},{25,17},{2,10},{10... | collective-permute-start | bytes 9437192 | tf_op jit(solution)/shard_map/ppermute | solution.py:66
  256.8 20.4 %collective-permute-start.34 = (bf16[2,2,48,2048]{3,2,0,1:T(8,128)(2,1)S(1)}, bf16[2,2,48,2048]{3,2,0,1:T(8,128)(2,1)S(1)}, u32[]{:S(2)}, u32[]{:S(2)}) collective-permute-start(bf16[2,2,48,2048]{3,2,0,1:T(8,128)(2,1)S(1)} %bitcast.414), channel_id=1, source_target_pairs={{0,16},{8,24},{16,0},{24,8},{1,17},{9,25},{17,1},{25,9},{2,18},{10... | collective-permute-start | bytes 2359304 | tf_op jit(solution)/shard_map/ppermute | solution.py:70
  268.9 25.3 %collective-permute-start.23 = (bf16[2,2,48,2048]{3,2,0,1:T(8,128)(2,1)}, bf16[2,2,48,2048]{3,2,0,1:T(8,128)(2,1)}, u32[]{:S(2)}, u32[]{:S(2)}) collective-permute-start(bf16[2,2,48,2048]{3,2,0,1:T(8,128)(2,1)} %pad_maximum_fusion.13), channel_id=1, source_target_pairs={{0,16},{8,24},{16,0},{24,8},{1,17},{9,25},{17,1},{25,9},{2,18},{10... | collective-permute-start | bytes 2359304 | tf_op jit(solution)/shard_map/ppermute | solution.py:70
  278.2 107.8 %collective-permute-start.35 = (bf16[768,2048]{1,0:T(8,128)(2,1)}, bf16[768,2048]{1,0:T(8,128)(2,1)}, u32[]{:S(2)}, u32[]{:S(2)}) collective-permute-start(bf16[768,2048]{1,0:T(8,128)(2,1)} %bitcast.133), channel_id=1, source_target_pairs={{0,8},{8,0},{16,24},{24,16},{1,9},{9,1},{17,25},{25,17},{2,10},{10... | collective-permute-start | bytes 9437192 | tf_op jit(solution)/shard_map/ppermute | solution.py:66
  279.5 31.5 %collective-permute-start.22 = (bf16[2,2,48,2048]{3,2,0,1:T(8,128)(2,1)S(1)}, bf16[2,2,48,2048]{3,2,0,1:T(8,128)(2,1)S(1)}, u32[]{:S(2)}, u32[]{:S(2)}) collective-permute-start(bf16[2,2,48,2048]{3,2,0,1:T(8,128)(2,1)S(1)} %pad_maximum_fusion.12), channel_id=1, source_target_pairs={{0,16},{8,24},{16,0},{24,8},{1,17},{9,25},{17,1},{25,9},{2,18},{10... | collective-permute-start | bytes 2359304 | tf_op jit(solution)/shard_map/ppermute | solution.py:70
  297.0 25.9 %collective-permute-start.24 = (bf16[2,128,2048]{2,1,0:T(8,128)(2,1)S(1)}, bf16[2,128,2048]{2,1,0:T(8,128)(2,1)S(1)}, u32[]{:S(2)}, u32[]{:S(2)}) collective-permute-start(bf16[2,128,2048]{2,1,0:T(8,128)(2,1)S(1)} %convolution_convert_fusion.9), channel_id=1, source_target_pairs={{0,6},{2,0},{4,2},{6,4},{1,7},{3,1},{5,3},{7,5},{8,14},{10,8},{12,... | collective-permute-start | bytes 3145736 | tf_op jit(solution)/shard_map/ppermute | solution.py:73
  303.5 30.0 %collective-permute-start.21 = (bf16[2,2,48,2048]{3,2,0,1:T(8,128)(2,1)}, bf16[2,2,48,2048]{3,2,0,1:T(8,128)(2,1)}, u32[]{:S(2)}, u32[]{:S(2)}) collective-permute-start(bf16[2,2,48,2048]{3,2,0,1:T(8,128)(2,1)} %pad_maximum_fusion.11), channel_id=1, source_target_pairs={{0,16},{8,24},{16,0},{24,8},{1,17},{9,25},{17,1},{25,9},{2,18},{10... | collective-permute-start | bytes 2359304 | tf_op jit(solution)/shard_map/ppermute | solution.py:70
  324.3 25.6 %collective-permute-start.25 = (bf16[2,128,2048]{2,1,0:T(8,128)(2,1)}, bf16[2,128,2048]{2,1,0:T(8,128)(2,1)}, u32[]{:S(2)}, u32[]{:S(2)}) collective-permute-start(bf16[2,128,2048]{2,1,0:T(8,128)(2,1)} %add_convert_fusion.2), channel_id=1, source_target_pairs={{0,6},{2,0},{4,2},{6,4},{1,7},{3,1},{5,3},{7,5},{8,14},{10,8},{12,... | collective-permute-start | bytes 3145736 | tf_op jit(solution)/shard_map/ppermute | solution.py:73
  330.8 50.0 %collective-permute-start.20 = (bf16[2,2,48,2048]{3,2,0,1:T(8,128)(2,1)}, bf16[2,2,48,2048]{3,2,0,1:T(8,128)(2,1)}, u32[]{:S(2)}, u32[]{:S(2)}) collective-permute-start(bf16[2,2,48,2048]{3,2,0,1:T(8,128)(2,1)} %pad_maximum_fusion.10), channel_id=1, source_target_pairs={{0,16},{8,24},{16,0},{24,8},{1,17},{9,25},{17,1},{25,9},{2,18},{10... | collective-permute-start | bytes 2359304 | tf_op jit(solution)/shard_map/ppermute | solution.py:70
  334.9 22.0 %copy-start.21 = (pred[16,2,48,128]{3,2,0,1:T(8,128)(4,1)S(1)}, pred[16,2,48,128]{3,2,0,1:T(8,128)(4,1)}, u32[]{:S(2)}) copy-start(pred[16,2,48,128]{3,2,0,1:T(8,128)(4,1)} %fusion.31) | copy-start | bytes 589828
  335.0 22.2 %copy-start.24 = (s32[16]{0:T(128)S(1)}, s32[16]{0:T(128)}, u32[]{:S(2)}) copy-start(s32[16]{0:T(128)} %get-tuple-element.108) | copy-start | bytes 196
  352.7 29.7 %collective-permute-start.26 = (bf16[2,128,2048]{2,1,0:T(8,128)(2,1)}, bf16[2,128,2048]{2,1,0:T(8,128)(2,1)}, u32[]{:S(2)}, u32[]{:S(2)}) collective-permute-start(bf16[2,128,2048]{2,1,0:T(8,128)(2,1)} %add_convert_fusion.1), channel_id=1, source_target_pairs={{0,6},{2,0},{4,2},{6,4},{1,7},{3,1},{5,3},{7,5},{8,14},{10,8},{12,... | collective-permute-start | bytes 3145736 | tf_op jit(solution)/shard_map/ppermute | solution.py:73
  358.0 21.0 %all-to-all-start = ((bf16[16,1,128]{2,1,0:T(2,128)(2,1)}), bf16[16,1,128]{2,1,0:T(2,128)(2,1)S(1)}, u32[]{:S(2)}, u32[]{:S(2)}) async-start(bf16[16,1,128]{2,1,0:T(2,128)(2,1)} %copy.171), calls=%async_computation | async-start | bytes 16384 | tf_op jit(solution)/shard_map/all_to_all | solution.py:230
  361.7 17.3 %copy-start.23 = (s32[128,8]{0,1:T(8,128)S(1)}, s32[128,8]{0,1:T(8,128)}, u32[]{:S(2)}) copy-start(s32[128,8]{0,1:T(8,128)} %param.8) | copy-start | bytes 12292
  384.5 20.8 %collective-permute-start.27 = (bf16[128,2048]{1,0:T(8,128)(2,1)S(1)}, bf16[128,2048]{1,0:T(8,128)(2,1)S(1)}, u32[]{:S(2)}, u32[]{:S(2)}) collective-permute-start(bf16[128,2048]{1,0:T(8,128)(2,1)S(1)} %slice_bitcast_fusion.4), channel_id=1, source_target_pairs={{0,1},{1,0},{2,3},{3,2},{4,5},{5,4},{6,7},{7,6},{8,9},{9,8},{10,11... | collective-permute-start | bytes 1572872 | tf_op jit(solution)/shard_map/ppermute | solution.py:63
  386.1 20.4 %copy-start.1 = (bf16[1,1,768,1536]{3,2,1,0:T(8,128)(2,1)S(1)}, bf16[1,1,768,1536]{3,2,1,0:T(8,128)(2,1)}, u32[]{:S(2)}) copy-start(bf16[1,1,768,1536]{3,2,1,0:T(8,128)(2,1)} %param.10) | copy-start | bytes 7077892
  (19 other events, 119.9 us)
